TPU v7x, 32 devices: a whole 2x2x4 slice. The times are simulated.
32 devices in a mesh: dp: 8 (over y, x, core), seq: 4 (over z).
Axes of the slice: x: 2, y: 2, z: 4, core: 2. Of those that a mesh axis runs over, the one named last changes fastest.
Arguments:
- dec_in: bfloat16 [24, 128, 1024], P('dp', 'seq'), may hold values from -6 to 6
- memory: bfloat16 [24, 7, 128, 1024], P('dp', None, 'seq'), may hold values from -6 to 6
- proj_w: bfloat16 [6, 1024, 1024], P(None, ('dp', 'seq')), may hold values from -0.1875 to 0.1875
- out_w: bfloat16 [2, 1024, 1024], P(None, ('dp', 'seq')), may hold values from -1.25 to 1.25
- ffn_in: bfloat16 [1024, 4096], P(('dp', 'seq')), may hold values from -0.1875 to 0.1875
- ffn_out: bfloat16 [4096, 1024], P(('dp', 'seq')), may hold values from -0.09375 to 0.09375
- biases: float32 [6, 1024], replicated, may hold values from -2 to 2
- out_bias: float32 [1024], replicated, may hold values from -2 to 2
- ffn_bias: float32 [4096], replicated, may hold values from -2 to 2
- norm_gain: float32 [3, 1024], replicated, may hold values from 0.5 to 1.5
- norm_bias: float32 [3, 1024], replicated, may hold values from -2 to 2
- mem_len: int32 [24], replicated, may hold values from 4 to 896, as said below
- dec_len: int32 [24], replicated, may hold values from 64 to 128, as said below
- mem_seg: int32 [24, 7, 128], P('dp'), may hold values from 0 to 3, as said below
- dec_seg: int32 [24, 128], P('dp'), may hold values from 0 to 3, as said below
- cotangent: bfloat16 [24, 128, 1024], P('dp', 'seq'), may hold values from -6 to 6
Outputs:
- mixed: bfloat16 [24, 128, 1024], P('dp', 'seq')
- d_dec: float32 [24, 128, 1024], P('dp', 'seq')
- d_memory: bfloat16 [24, 7, 128, 1024], P('dp', None, 'seq')
- g_proj: float32 [6, 1024, 1024], P(None, 'seq')
- g_out: float32 [2, 1024, 1024], P(None, 'seq')
- g_ffn_in: float32 [1024, 4096], P('seq')
- g_ffn_out: float32 [4096, 1024], P('seq')
- g_biases: float32 [6, 1024], P(None, 'seq')
- g_out_bias: float32 [1024], P('seq')
- g_ffn_bias: float32 [4096], P('seq')
- g_gain: float32 [3, 1024], P(None, 'seq')
- g_shift: float32 [3, 1024], P(None, 'seq')
Inputs may be any that keep to these rules, and one draw needn't show every extreme that they name: Memory slots 0 to mem_len - 1 of a row are live. With tiles of 128 slots a row has ceil(mem_len / 128) live tiles; the 24 rows together have exactly 96, and in every draw the 3 rows of some index of dp have 3 * 7. Decoder slots 0 to dec_len - 1 of a row are live; every index of dp holds a row with dec_len = 128. `mem_seg`: along a row's slots (tile, then position) never falling, from 0 to the row's pair count minus 1, each of these values on some live slot; slots past mem_len hold the last. `dec_seg`: along a row never falling, with the same pair count as the row's mem_seg, each value on some live slot; slots past dec_len hold the last. Every index of dp holds a row whose dec_seg is 0 throughout and whose dec_len is 128.
All inputs are finite; a program needn't handle non-finite values.
Results may differ from a plain program's by a relative error of at most 0.023.
Values may be sent and summed in bfloat16 or wider, within the bound.
No kernel may reach another device: no remote copies, remote signals or barrier semaphores. Data moves between devices by JAX's collectives and lax.ppermute only.
A program may use at most 320 MiB of HBM per device.

v0:
```python
import functools

import jax
import jax.numpy as jnp
from jax import lax
from jax.experimental import pallas as pl
from jax.experimental.pallas import tpu as pltpu
from jax.sharding import Mesh
from jax.sharding import PartitionSpec as P

HEADS = 16
HEAD_DIM = 64
LOCAL_HEADS = 4
EPS = 1e-05
NEG = -1e30
F32 = jnp.float32
BF16 = jnp.bfloat16
AXES = ("hi", "x", "core", "z")
ORDER = (0, 2, 1, 3)
VMEM_LIMIT = 60 * 1024 * 1024


def mm(left, right):
    return jnp.dot(left, right, preferred_element_type=F32)


def mm_t(left, right):
    return lax.dot_general(left, right, (((1,), (1,)), ((), ())), preferred_element_type=F32)


def t_mm(left, right):
    return lax.dot_general(left, right, (((0,), (0,)), ((), ())), preferred_element_type=F32)


def pick(array, index, axis=0):
    return lax.dynamic_index_in_dim(array, index, axis, False)


def swap(values, axis):
    return lax.ppermute(values, axis, [(0, 1), (1, 0)])


def head_masks(width):
    lane = lax.broadcasted_iota(jnp.int32, (1, width), 1)
    return [(lane // HEAD_DIM) == h for h in range(LOCAL_HEADS)]


def stack_heads(values, masks):
    zero = jnp.zeros_like(values)
    return jnp.concatenate([jnp.where(m, values, zero) for m in masks], 0)


def join_heads(stacked, masks, rows):
    out = jnp.zeros((rows, stacked.shape[1]), stacked.dtype)
    for h, m in enumerate(masks):
        out = jnp.where(m, stacked[h * rows : (h + 1) * rows], out)
    return out


def softmax_parts(scores, allowed):
    scores = jnp.where(allowed, scores * HEAD_DIM**-0.5, NEG)
    top = jnp.max(scores, -1, keepdims=True)
    expo = jnp.exp(scores - top)
    return expo * (1.0 / jnp.sum(expo, -1, keepdims=True))


def attend_core(q, k, v, allowed):
    rows, width = q.shape
    masks = head_masks(width)
    scores = mm_t(stack_heads(q, masks), k)
    probs = [
        softmax_parts(scores[h * rows : (h + 1) * rows], allowed).astype(BF16)
        for h in range(LOCAL_HEADS)
    ]
    mixed = mm(jnp.concatenate(probs, 0), v)
    return join_heads(mixed, masks, rows).astype(BF16)


def attend_back_core(q, k, v, allowed, grad):
    rows, width = q.shape
    masks = head_masks(width)
    q_heads = stack_heads(q, masks)
    grad_heads = stack_heads(grad, masks)
    scores = mm_t(q_heads, k)
    grad_probs = mm_t(grad_heads, v)
    probs, grad_scores = [], []
    for h in range(LOCAL_HEADS):
        part = slice(h * rows, (h + 1) * rows)
        p = softmax_parts(scores[part], allowed)
        gp = grad_probs[part]
        centre = jnp.sum(p * gp, -1, keepdims=True)
        grad_scores.append((p * (gp - centre)).astype(BF16))
        probs.append(p.astype(BF16))
    probs = jnp.concatenate(probs, 0)
    grad_scores = jnp.concatenate(grad_scores, 0)
    scale = HEAD_DIM**-0.5
    dq = join_heads(mm(grad_scores, k), masks, rows) * scale
    dk = t_mm(grad_scores, q_heads) * scale
    dv = t_mm(probs, grad_heads)
    return dq.astype(BF16), dk.astype(BF16), dv.astype(BF16)


KERNEL_US = {
    "cut_cols_kernel": 2,
    "pack_kernel": 2,
    "pack_ffn_kernel": 2,
    "place_kernel": 4,
    "self_fwd_kernel": 5,
    "norm_one_kernel": 3,
    "memory_kv_kernel": 7,
    "cross_fwd_kernel": 8,
    "norm_two_kernel": 3,
    "place_ffn_kernel": 5,
    "ffn_fwd_kernel": 6,
    "norm_three_kernel": 3,
    "ffn_bwd_kernel": 6,
    "ffn_grad_kernel": 6,
    "norm_back_kernel": 3,
    "cross_bwd_kernel": 11,
    "memory_grad_kernel": 9,
    "cross_grad_kernel": 4,
    "self_bwd_kernel": 6,
    "self_grad_kernel": 5,
    "memory_back_kernel": 8,
    "pair_sum_kernel": 3,
    "final_sum_kernel": 2,
    "join_kernel": 1,
    "proj_out_kernel": 7,
    "ffn_out_kernel": 6,
    "small_kernel": 1,
}


def run(kernel, args, outs, scratch=(), aliases=None, any_args=(), any_outs=()):
    single = not isinstance(outs, (list, tuple))
    out_list = [outs] if single else list(outs)
    vmem = pl.BlockSpec(memory_space=pltpu.VMEM)
    anywhere = pl.BlockSpec(memory_space=pl.ANY)
    base = getattr(kernel, "func", kernel)
    result = pl.pallas_call(
        kernel,
        name=base.__name__,
        in_specs=[anywhere if i in any_args else vmem for i in range(len(args))],
        out_specs=[anywhere if i in any_outs else vmem for i in range(len(out_list))],
        out_shape=out_list,
        scratch_shapes=list(scratch),
        input_output_aliases=aliases or {},
        cost_estimate=pl.CostEstimate(
            flops=KERNEL_US[base.__name__] * 1_100_000_000, bytes_accessed=0, transcendentals=0
        ),
        compiler_params=pltpu.CompilerParams(vmem_limit_bytes=VMEM_LIMIT),
    )(*args)
    return result[0] if single else result


def shaped(shape, dtype):
    return jax.ShapeDtypeStruct(shape, dtype)


def group_place():
    return lax.axis_index("x") * 2 + lax.axis_index("core")


def lanes(start, size):
    return pl.ds(pl.multiple_of(start, 128), size)


def local_bias(ref, row, j, parts=2):
    n = ref.shape[1]
    size = n // (4 * parts)
    return jnp.concatenate(
        [ref[pl.ds(row, 1), lanes(p * 4 * size + j * size, size)] for p in range(parts)], 1
    )


def whole(refs):
    return jnp.concatenate([r[...] for r in refs], 0)


def halves(product, act, sent_ref, kept_ref):
    half = act.shape[0] // 2
    sent_ref[...] = product(act[half:]).astype(BF16)
    kept_ref[...] = product(act[:half])


def flat_row(ref, r):
    block = ref[:, r]
    return block.reshape(block.shape[0] * block.shape[1], block.shape[2])


def self_fwd_kernel(x0, x1, x2, x3, w, wo, biases, mask, qkv_out, o_out, sent, kept):
    j = group_place()
    tokens = whole([x0, x1, x2, x3])
    width = wo.shape[0]
    bq = local_bias(biases, 0, j)
    bias = jnp.concatenate([bq, jnp.zeros_like(bq), local_bias(biases, 1, j)], 1)
    qkv = (mm(tokens, w[...]) + bias).astype(BF16)
    qkv_out[...] = qkv.reshape(qkv_out.shape)
    for r in range(qkv_out.shape[1]):
        row = flat_row(qkv_out, r)
        out = attend_core(
            row[:, :width], row[:, width : 2 * width], row[:, 2 * width :], mask[r] > 0.5
        )
        o_out[:, r] = out.reshape(o_out.shape[0], o_out.shape[2], width)
    mixed = o_out[...].reshape(tokens.shape[0], width)
    halves(lambda a: mm(a, wo[...]), mixed, sent, kept)


def cross_allowed(qc, kc):
    return (kc >= 0.0) & ((kc == qc) | (qc < -1.5))


def memory_kv_kernel(m0, m1, m2, m3, w, biases, *outs):
    j = group_place()
    width = w.shape[1] // 3
    bv = local_bias(biases, 3, j)
    bias = jnp.concatenate([jnp.zeros_like(bv), bv], 1)
    for r, out in enumerate(outs):
        mem = jnp.concatenate([m[r] for m in (m0, m1, m2, m3)], 0)
        out[...] = (mm(mem, w[:, width:]) + bias).astype(BF16)


def memory_back_kernel(*refs):
    dkvs, (w, sent, kept) = refs[:-3], refs[-3:]
    width = w.shape[1] // 3
    for r, dkv in enumerate(dkvs):
        slots = dkv.shape[0] // 4
        far = mm_t(dkv[2 * slots :], w[:, width:]).astype(BF16)
        near = mm_t(dkv[: 2 * slots], w[:, width:])
        for d in range(2):
            sent[d, r] = far[d * slots : (d + 1) * slots]
            kept[d, r] = near[d * slots : (d + 1) * slots]


def cross_fwd_kernel(rows, *refs):
    h, (w, wo, biases), kvs = refs[:4], refs[4:7], refs[7 : 7 + rows]
    q_code, k_code, q_out, o_out, sent, kept = refs[7 + rows :]
    tokens = whole(h)
    width = wo.shape[0]
    query = (mm(tokens, w[:, :width]) + local_bias(biases, 2, group_place())).astype(BF16)
    q_out[...] = query.reshape(q_out.shape)
    for r, kv in enumerate(kvs):
        allowed = cross_allowed(q_code[r], k_code[r])
        out = attend_core(flat_row(q_out, r), kv[:, :width], kv[:, width:], allowed)
        o_out[:, r] = out.reshape(o_out.shape[0], o_out.shape[2], width)
    mixed = o_out[...].reshape(tokens.shape[0], width)
    halves(lambda a: mm(a, wo[...]), mixed, sent, kept)


def ffn_fwd_kernel(h0, h1, h2, h3, w1, w2, bias, g_out, slope_out, sent, kept):
    j = group_place()
    tokens = whole([h0, h1, h2, h3])
    u = mm(tokens, w1[...]) + local_bias(bias, 0, j, 4)
    normal = 0.5 * (1.0 + lax.erf(u * 0.7071067811865476))
    slope_out[...] = normal + u * (0.3989422804014327 * jnp.exp(-0.5 * u * u))
    g_out[...] = (u * normal).astype(BF16)
    halves(lambda a: mm(a, w2[...]), g_out[...], sent, kept)


def ffn_bwd_kernel(f0, f1, f2, f3, w1, w2, slope, du_out, bias_out, sent, kept):
    grads = whole([f0, f1, f2, f3])
    du = (mm_t(grads, w2[...]) * slope[...]).astype(BF16)
    du_out[...] = du
    bias_out[...] = jnp.sum(du.astype(F32), 0, keepdims=True)
    halves(lambda a: mm_t(a, w1[...]), du, sent, kept)


def cross_bwd_kernel(rows, *refs):
    f, (w, wo, q), kvs = refs[:4], refs[4:7], refs[7 : 7 + rows]
    q_code, k_code, dq_out = refs[7 + rows : 10 + rows]
    dkvs = refs[10 + rows : 10 + 2 * rows]
    sums, sent, kept, do_ref = refs[10 + 2 * rows :]
    grads = whole(f)
    width = wo.shape[0]
    do_ref[...] = mm_t(grads, wo[...]).astype(BF16).reshape(do_ref.shape)
    total_v = jnp.zeros((1, width), F32)
    for r, (kv, dkv) in enumerate(zip(kvs, dkvs)):
        allowed = cross_allowed(q_code[r], k_code[r])
        dq, dk, dv = attend_back_core(
            flat_row(q, r), kv[:, :width], kv[:, width:], allowed, flat_row(do_ref, r)
        )
        dq_out[:, r] = dq.reshape(dq_out.shape[0], dq_out.shape[2], width)
        dkv[:, :width] = dk
        dkv[:, width:] = dv
        total_v = total_v + jnp.sum(dv.astype(F32), 0, keepdims=True)
    dq = dq_out[...].reshape(grads.shape[0], width)
    total_q = jnp.sum(dq.astype(F32), 0, keepdims=True)
    sums[...] = jnp.concatenate([total_q, total_v, jnp.zeros((6, width), F32)], 0)
    halves(lambda a: mm_t(a, w[:, :width]), dq, sent, kept)


def self_bwd_kernel(f0, f1, f2, f3, w, wo, qkv, mask, dqkv_out, sums, sent, kept):
    grads = whole([f0, f1, f2, f3])
    width = wo.shape[0]
    shape = (qkv.shape[0], qkv.shape[1], qkv.shape[2], width)
    do = mm_t(grads, wo[...]).astype(BF16).reshape(shape)
    for r in range(shape[1]):
        row = flat_row(qkv, r)
        grad = do[:, r].reshape(row.shape[0], width)
        parts = attend_back_core(
            row[:, :width], row[:, width : 2 * width], row[:, 2 * width :], mask[r] > 0.5, grad
        )
        dqkv_out[:, r] = jnp.concatenate(parts, 1).reshape(shape[0], shape[2], 3 * width)
    dqkv = dqkv_out[...].reshape(grads.shape[0], 3 * width)
    sums[...] = jnp.sum(dqkv.astype(F32), 0, keepdims=True)
    halves(lambda a: mm_t(a, w[...]), dqkv, sent, kept)


def branch_sum(kept, arrived, crossed):
    n = crossed.shape[0]
    return kept[:n] + arrived[:n].astype(F32) + crossed[...].astype(F32)


def normalise(v):
    centre = v - jnp.mean(v, -1, keepdims=True)
    rstd = lax.rsqrt(jnp.mean(centre * centre, -1, keepdims=True) + EPS)
    return centre * rstd, rstd


def denormalise(e, gain, n, rstd):
    a = e * gain
    return rstd * (a - jnp.mean(a, -1, keepdims=True) - n * jnp.mean(a * n, -1, keepdims=True))


def norm_one_kernel(kept, arrived, crossed, own, bias, gains, shifts, n_out, rstd_out, low_out):
    v = branch_sum(kept, arrived, crossed) + bias[...] + own[...].astype(F32)
    n, rstd = normalise(v)
    n_out[...] = n
    rstd_out[...] = jnp.broadcast_to(rstd, rstd_out.shape)
    low_out[...] = (n * gains[0:1] + shifts[0:1]).astype(BF16)


def norm_two_kernel(kept, arrived, crossed, n_one, biases, gains, shifts, n_out, rstd_out, low_out):
    resid = n_one[...] * gains[0:1] + shifts[0:1]
    n, rstd = normalise(branch_sum(kept, arrived, crossed) + biases[4:5] + resid)
    n_out[...] = n
    rstd_out[...] = jnp.broadcast_to(rstd, rstd_out.shape)
    low_out[...] = (n * gains[1:2] + shifts[1:2]).astype(BF16)


def sums_of(e, n, low):
    return jnp.concatenate(
        [
            jnp.sum(e * n, 0, keepdims=True),
            jnp.sum(e, 0, keepdims=True),
            jnp.sum(low.astype(F32), 0, keepdims=True),
            jnp.zeros((5, e.shape[1]), F32),
        ],
        0,
    )


def norm_three_kernel(
    kept, arrived, crossed, n_two, biases, gains, shifts, cot, live, mixed_out, d_out, low_out, sums
):
    resid = n_two[...] * gains[1:2] + shifts[1:2]
    n, rstd = normalise(branch_sum(kept, arrived, crossed) + biases[5:6] + resid)
    mixed_out[...] = ((n * gains[2:3] + shifts[2:3]) * live[...]).astype(BF16)
    e = cot[...].astype(F32) * live[...]
    d = denormalise(e, gains[2:3], n, rstd)
    low = d.astype(BF16)
    d_out[...] = d
    low_out[...] = low
    sums[...] = sums_of(e, n, low)


def norm_back_kernel(which, kept, arrived, crossed, d_in, n, rstd, gains, d_out, low_out, sums):
    e = branch_sum(kept, arrived, crossed) + d_in[...]
    d = denormalise(e, gains[which : which + 1], n[...], rstd[:, 0:1])
    low = d.astype(BF16)
    d_out[...] = d
    low_out[...] = low
    sums[...] = sums_of(e, n[...], low)


def cut_cols_kernel(proj, first, *outs):
    j = group_place()
    n, _, width = proj.shape
    ff = first.shape[1]
    for d, out in enumerate(outs):
        target = jnp.bitwise_xor(j, d)
        at = 0
        for m in range(n):
            for h in range(2):
                out[:, at : at + width // 8] = proj[
                    m, :, lanes(h * (width // 2) + target * (width // 8), width // 8)
                ]
                at += width // 8
        for q in range(4):
            size = ff // 16
            out[:, at : at + size] = first[:, lanes(q * (ff // 4) + target * size, size)]
            at += size


def pack_kernel(e0, e1, e2, e3, out_w, buf_ab):
    j = group_place()
    quarter = out_w.shape[2] // 4
    six = 6 * quarter
    for d, e in enumerate([e0, e1, e2, e3]):
        buf_ab[jnp.bitwise_xor(j, d), :, :six] = e[:, :six]
    for i in range(4):
        for m in range(2):
            at = six + m * quarter
            buf_ab[i, :, at : at + quarter] = out_w[m, :, i * quarter : (i + 1) * quarter]


def pack_ffn_kernel(e0, e1, e2, e3, second, buf_c):
    j = group_place()
    rows, cols = buf_c.shape[1], buf_c.shape[2]
    for d, e in enumerate([e0, e1, e2, e3]):
        buf_c[jnp.bitwise_xor(j, d)] = e[:, e.shape[1] - cols :]
    for i in range(4):
        buf_c[4 + i] = second[i * rows : (i + 1) * rows]


def place_kernel(blocks, w_qkv, w_two, w_out, w_out2):
    cols = w_qkv.shape[-1]
    quarter = cols // 3
    for h in range(blocks.shape[0]):
        for z in range(blocks.shape[1]):
            for i in range(4):
                w_qkv[h, i, z] = blocks[h, z, i, :, :cols]
                w_two[h, i, z] = blocks[h, z, i, :, cols : 2 * cols]
                for m, out in enumerate([w_out, w_out2]):
                    at = 2 * cols + m * quarter
                    out[h, z, :, i * quarter : (i + 1) * quarter] = blocks[
                        h, z, i, :, at : at + quarter
                    ]


def place_ffn_kernel(blocks, wcol, wrow):
    rows = wcol.shape[-2]
    for h in range(blocks.shape[0]):
        for z in range(blocks.shape[1]):
            for i in range(4):
                wcol[h, i, z] = blocks[h, z, i]
                wrow[h, z, i * rows : (i + 1) * rows] = blocks[h, z, 4 + i]


def select_rows(dst, pieces, n_z, half_index):
    z = lax.axis_index("z")
    at = 0
    for piece in pieces:
        count, width = piece.shape
        for k in range(n_z):
            start = lax.rem(z + k, n_z) * (width // n_z) + half_index * (width // n_z // 2)
            dst[at : at + count, k * 128 : (k + 1) * 128] = piece[:, lanes(start, 128)]
        at += count


def select_cols(dst, pieces, n_z):
    z = lax.axis_index("z")
    at = 0
    for piece in pieces:
        count, width = piece.shape
        size = width // n_z
        for k in range(n_z):
            start = lax.rem(z + k, n_z) * size
            dst[at : at + count, k * size : (k + 1) * size] = piece[:, lanes(start, size)]
        at += count


def put_cols(out, at, block):
    n_z, rows = out.shape[0], out.shape[1]
    cols = block.shape[1]
    out[:, :, at : at + cols] = block.astype(BF16).reshape(n_z, rows, cols)


def put_rows(out, at, block):
    n_z, rows = out.shape[0], out.shape[1]
    size = block.shape[1] // n_z
    for k in range(n_z):
        for i in range(block.shape[0] // rows):
            out[k, :, at + i * size : at + (i + 1) * size] = block[
                i * rows : (i + 1) * rows, k * size : (k + 1) * size
            ].astype(BF16)


def half_of(ref, h):
    size = ref.shape[1] // 2
    return ref[:, lanes(h * size, size)]


def ffn_grad_kernel(a0, a1, a2, a3, du, g, f0, f1, f2, f3, out):
    n_hi, n_z, rows = out.shape[0], out.shape[1], out.shape[2]
    cols = du.shape[1]
    first = t_mm(whole([a0, a1, a2, a3]), du[...]).astype(BF16)
    second = t_mm(g[...], whole([f0, f1, f2, f3])).astype(BF16)
    for z in range(n_z):
        for h in range(n_hi):
            at = (z * n_hi + h) * rows
            out[h, z, :, :cols] = first[at : at + rows]
            out[h, z, :, cols:] = second[at : at + rows]


def memory_grad_kernel(n_z, rows, *refs):
    mems, dkvs, (kept, sent, left) = refs[:4], refs[4 : 4 + rows], refs[4 + rows :]
    hi = lax.axis_index("hi")
    for out, h in ((sent, 1 - hi), (kept, hi)):
        total = 0.0
        for r in range(rows):
            select_rows(left, [m.at[r] for m in mems], n_z, h)
            total = total + t_mm(left[...], dkvs[r][...])
        put_cols(out, 0, total)


def cross_grad_kernel(
    n_z, h0, h1, h2, h3, dq, kv_kept, kv_sent, o2, f0, f1, f2, f3, kept, sent, left, right
):
    hi = lax.axis_index("hi")
    c_q, c_kv = dq.shape[1], kv_kept.shape[2]
    select_cols(right, [f0, f1, f2, f3], n_z)
    for out, h, kv in ((sent, 1 - hi, kv_sent), (kept, hi, kv_kept)):
        select_rows(left, [h0, h1, h2, h3], n_z, h)
        put_cols(out, 0, t_mm(left[...], dq[...]))
        out[:, :, c_q : c_q + c_kv] = kv[...]
        put_rows(out, c_q + c_kv, t_mm(half_of(o2, h), right[...]))


def self_grad_kernel(
    n_z, x0, x1, x2, x3, dqkv, sums, small, o1, f0, f1, f2, f3, kept, sent, left, right
):
    hi = lax.axis_index("hi")
    rows = kept.shape[1] - 16
    cols = dqkv.shape[1]
    last = jnp.concatenate([sums[...], jnp.zeros((1, right.shape[1] - cols), F32)], 1)
    at_last = lax.broadcasted_iota(jnp.int32, small.shape, 0) == small.shape[0] - 1
    lower = jnp.where(at_last, last, small[...]).astype(BF16)
    select_cols(right, [f0, f1, f2, f3], n_z)
    size = right.shape[1] // n_z
    for out, h in ((sent, 1 - hi), (kept, hi)):
        select_rows(left, [x0, x1, x2, x3], n_z, h)
        block = t_mm(left[...], dqkv[...]).astype(BF16)
        other = t_mm(half_of(o1, h), right[...]).astype(BF16)
        for k in range(n_z):
            out[k, :rows, :cols] = block[k * rows : (k + 1) * rows]
            out[k, rows:] = lower
            out[k, :rows, cols:] = other[:, k * size : (k + 1) * size]


def pair_sum_kernel(kept, arrived, own, *sent):
    own[...] = kept[0].astype(F32) + arrived[0].astype(F32)
    for k, out in enumerate(sent):
        out[...] = (kept[k + 1].astype(F32) + arrived[k + 1].astype(F32)).astype(BF16)


def final_sum_kernel(cols, own, *refs):
    total = own[...]
    arrived, outs = refs[: -len(cols)], refs[-len(cols) :]
    for a in arrived:
        total = total + a[...].astype(F32)
    at = 0
    for out, size in zip(outs, cols):
        out[...] = total[:, at : at + size].astype(BF16)
        at += size


def places(index):
    h = jnp.bitwise_xor(lax.axis_index("hi"), (index >> 2) & 1)
    return h, jnp.bitwise_xor(group_place(), index & 3)


def ffn_out_kernel(*refs):
    pieces, first, second = refs[:8], refs[8], refs[9]
    rows = pieces[0].shape[0]
    ff = first.shape[1]
    size = ff // 16
    for index, piece in enumerate(pieces):
        h, j = places(index)
        at_rows = pl.ds(pl.multiple_of(h * rows, 8), rows)
        for q in range(4):
            first[at_rows, lanes(q * 4 * size + j * size, size)] = piece[
                :, q * size : (q + 1) * size
            ].astype(F32)
        second[pl.ds(pl.multiple_of((j * 2 + h) * rows, 8), rows), :] = piece[
            :, 4 * size :
        ].astype(F32)


def place_cols(out, m, rows, piece, at):
    width = out.shape[2]
    for index, p in enumerate(piece):
        h, j = places(index)
        for half in range(2):
            lo = at + half * (width // 8)
            out[
                m,
                pl.ds(pl.multiple_of(h * rows, 8), rows),
                lanes(half * (width // 2) + j * (width // 8), width // 8),
            ] = p[:rows, lo : lo + width // 8].astype(F32)


def place_rows(out, m, rows, pieces, at):
    size = out.shape[2] // 4
    for index, piece in enumerate(pieces):
        h, j = places(index)
        out[m, pl.ds(pl.multiple_of(h * rows, 8), rows), lanes(j * size, size)] = piece[
            :rows, at : at + size
        ].astype(F32)


def join_kernel(cols_b, cols_a, planed, rows_a, out):
    rows = cols_b.shape[0]
    c, r = cols_b.shape[1], rows_a.shape[1]
    out[...] = jnp.zeros_like(out)
    out[:rows, :c] = cols_b[...]
    out[:, c : 2 * c] = cols_a[...]
    out[:rows, 2 * c :] = planed[...]
    out[rows:, 2 * c : 2 * c + r] = rows_a[rows:, :]


def proj_out_kernel(n_z, *refs):
    pieces, (g_proj, g_out, g_biases, g_out_bias, g_ffn_bias, g_norms, sums, small) = (
        refs[:8],
        refs[8:],
    )
    rows = pieces[0].shape[0] - 16
    width = g_proj.shape[2]
    quarter = width // 4
    for m in range(3):
        place_cols(g_proj, m + 3, rows, pieces, m * quarter)
        place_cols(g_proj, m, rows, pieces, (3 + m) * quarter)
    place_rows(g_out, 1, rows, pieces, 6 * quarter)
    place_rows(g_out, 0, rows, pieces, 7 * quarter)
    lowers = [p[rows:, 3 * quarter : 7 * quarter].astype(F32) for p in pieces[:4]]
    small[...] = (lowers[0] + lowers[1]) + (lowers[2] + lowers[3])
    for index, lower in enumerate(lowers):
        _, j = places(index)
        for m in range(3):
            for half in range(2):
                lo = m * quarter + half * (width // 8)
                sums[m : m + 1, lanes(half * (width // 2) + j * (width // 8), width // 8)] = lower[
                    15:16, lo : lo + width // 8
                ]
    z = lax.axis_index("z")
    own = lanes(z * (width // n_z), width // n_z)
    ff_rows = n_z * g_ffn_bias.shape[1] // width
    g_biases[0:1] = sums[0:1, own]
    g_biases[1:2] = sums[2:3, own]
    g_biases[2:6] = small[0:4, own]
    g_out_bias[...] = small[4:5, own]
    g_ffn_bias[...] = small[pl.ds(5 + z * (ff_rows // n_z), 1), :]
    g_norms[...] = small[5 + ff_rows : 11 + ff_rows, own]


def small_kernel(s3, s2, s1, cross_sums, ff_sum, out):
    j = group_place()
    width = out.shape[1]
    ff = ff_sum.shape[1] * 4
    out[...] = jnp.zeros_like(out)
    for half in range(2):
        at = lanes(half * (width // 2) + j * (width // 8), width // 8)
        part = slice(half * (width // 8), (half + 1) * (width // 8))
        out[0:1, at] = cross_sums[0:1, part]
        out[1:2, at] = cross_sums[1:2, part]
    out[2:3] = s2[2:3]
    out[3:4] = s3[2:3]
    out[4:5] = s1[2:3]
    ff_rows = ff // width
    per = ff // 16
    for q in range(4):
        flat_at = q * (ff // 4) + j * per
        row = 5 + flat_at // width
        out[pl.ds(row, 1), lanes(lax.rem(flat_at, width), per)] = ff_sum[
            0:1, q * per : (q + 1) * per
        ]
    at = 5 + ff_rows
    for i, s in enumerate([s1, s2, s3]):
        out[at + i : at + i + 1] = s[0:1]
        out[at + 3 + i : at + 4 + i] = s[1:2]


def per_device(
    dec_in,
    memory,
    proj_w,
    out_w,
    ffn_in,
    ffn_out,
    biases,
    out_bias,
    ffn_bias,
    norm_gain,
    norm_bias,
    mem_len,
    dec_len,
    mem_seg,
    dec_seg,
    cotangent,
):
    n_hi = lax.axis_size("hi")
    n_z = lax.axis_size("z")
    hi = lax.axis_index("hi")
    zi = lax.axis_index("z")
    j = group_place()
    fast = n_hi == 2 and n_z == 4
    row_count, query_count, width = dec_in.shape
    tile_count, tile_part = memory.shape[1], memory.shape[2]
    own_tokens = row_count * query_count
    all_tokens = 4 * own_tokens
    slots = tile_count * tile_part
    ff_width = ffn_in.shape[1]
    local = width // 4
    ff_local = ff_width // 4

    def turned(index):
        return (index & 1) * 2 + (index >> 1)

    to_rows = [
        ((h * 4 + a) * 4 + b, (h * 4 + turned(b)) * 4 + turned(a))
        for h in range(n_hi)
        for a in range(4)
        for b in range(4)
    ]

    def transpose(values):
        return lax.ppermute(values, AXES, to_rows)

    def shift_z(values, k):
        return lax.ppermute(values, "z", [(i, (i + k) % n_z) for i in range(n_z)])

    def gather_j(values):
        across = swap(values, "x")
        return [values, across, swap(values, "core"), swap(across, "core")]

    def cross_links(sent, kept):
        arrived = swap(sent, "core")
        half = kept.shape[0] // 2
        middle = (kept[half:] + arrived[half:].astype(F32)).astype(BF16)
        return kept, arrived, swap(middle, "x")

    def add_crossed(kept, arrived, crossed, other=0.0):
        n = crossed.shape[0]
        total = kept[:n] + arrived[:n].astype(F32) + crossed.astype(F32) + other
        return total.astype(BF16)

    def split_cols(full, parts=2):
        n, total, cols = full.shape
        split = pick(full.reshape(n, total, parts, 4, cols // (4 * parts)), j, 3)
        return split.transpose(1, 0, 2, 3).reshape(total, n * cols // 4)

    def split_rows(full, parts=2):
        total, cols = full.shape
        split = full.reshape(parts, 4, total // (4 * parts), cols)
        return pick(split, j, 1).reshape(total // 4, cols)

    def near_blocks(block):
        return [block] + [shift_z(block, -k) for k in range(1, n_z)]

    def after(values, *others):
        return lax.optimization_barrier((values, *others))[0]

    segs = transpose(jnp.concatenate([mem_seg.reshape(row_count, -1), dec_seg], 1))
    own_in = transpose(dec_in).reshape(own_tokens, width)
    tokens = gather_j(own_in)
    own_memory = transpose(after(memory, own_in, segs)).reshape(row_count, slots, width)
    mems = gather_j(own_memory)
    if fast:
        rows = proj_w.shape[1]
        cut = shaped((rows, 6 * local + ff_local), BF16)
        e = run(cut_cols_kernel, [proj_w, ffn_in], [cut] * 4)
        diag = [(0, 3), (1, 2), (2, 1), (3, 0)]
        e = [e[0], swap(e[1], "core"), swap(e[2], "x"), lax.ppermute(e[3], ("x", "core"), diag)]
        to_quarter = [
            ((h * 4 + a) * 4 + b, (h * 4 + 2 * (a % 2) + b // 2) * 4 + 2 * (a // 2) + b % 2)
            for h in range(2)
            for a in range(4)
            for b in range(4)
        ]
        buf_ab = run(pack_kernel, e + [out_w], shaped((4, rows, 2 * width), BF16))
        second = lax.ppermute(after(ffn_out, own_memory), AXES, to_quarter)
        buf_c = run(pack_ffn_kernel, e + [second], shaped((8, rows, ff_local), BF16))
        all_ab = lax.all_gather(after(buf_ab, own_memory), ("hi", "z"), axis=0)
        col_shape = shaped((2, 4, n_z, rows, 3 * local), BF16)
        row_shape = shaped((2, n_z, rows, width), BF16)
        placed = run(
            place_kernel,
            [all_ab.reshape((2, n_z) + buf_ab.shape)],
            [col_shape, col_shape, row_shape, row_shape],
        )
        w_qkv, w_two = (w.reshape(-1, 3 * local) for w in placed[:2])
        w_out, w_out2 = (w.reshape(-1, width) for w in placed[2:])
        all_c = lax.all_gather(after(buf_c, all_ab), ("hi", "z"), axis=0)
        w_first, w_second = run(
            place_ffn_kernel,
            [all_c.reshape((2, n_z) + buf_c.shape)],
            [
                shaped((2, 4, n_z, rows, ff_local), BF16),
                shaped((2, n_z, ffn_out.shape[0], width), BF16),
            ],
        )
        w_first = w_first.reshape(-1, ff_local)
        w_second = w_second.reshape(-1, width)
    else:
        proj_full = lax.all_gather(proj_w, AXES, axis=1, tiled=True)
        out_full = lax.all_gather(out_w, AXES, axis=1, tiled=True)
        w_qkv, w_two = split_cols(proj_full[:3]), split_cols(proj_full[3:])
        w_out, w_out2 = split_rows(out_full[0]), split_rows(out_full[1])
        w_first = split_cols(lax.all_gather(ffn_in, AXES, axis=0, tiled=True)[None], 4)
        w_second = split_rows(lax.all_gather(ffn_out, AXES, axis=0, tiled=True), 4)

    own_cot = transpose(after(cotangent, mems[3])).reshape(own_tokens, width)
    mem_full = mem_seg.shape[1] * mem_seg.shape[2]
    group = hi * 4 + turned(zi)
    own_dlen = lax.dynamic_slice_in_dim(dec_len, group * row_count, row_count)
    own_mlen = lax.dynamic_slice_in_dim(mem_len, group * row_count, row_count)
    parts = [turned(j ^ d) for d in ORDER]
    mem_parts = segs[:, :mem_full].reshape(row_count, tile_count, 4, tile_part)
    dec_parts = segs[:, mem_full:].reshape(row_count, 4, query_count)
    dseg = jnp.concatenate([pick(dec_parts, p, 1) for p in parts], 1)
    mseg = jnp.concatenate([pick(mem_parts, p, 2).reshape(row_count, slots) for p in parts], 1)
    dpos = jnp.concatenate([p * query_count + jnp.arange(query_count) for p in parts])
    in_tile = jnp.arange(tile_count)[:, None] * (4 * tile_part) + jnp.arange(tile_part)[None, :]
    mpos = jnp.concatenate([(in_tile + p * tile_part).reshape(-1) for p in parts])
    dlive = dpos[None, :] < own_dlen[:, None]
    mlive = mpos[None, :] < own_mlen[:, None]
    self_mask = (
        (dseg[:, :, None] == dseg[:, None, :])
        & (dpos[None, None, :] <= dpos[None, :, None])
        & dlive[:, None, :]
    ) | (dpos[None, None, :] == dpos[None, :, None])
    self_mask = self_mask.astype(F32)
    q_code = jnp.where(dlive, dseg.astype(F32), -2.0)[:, :, None]
    k_code = jnp.where(mlive, mseg.astype(F32), -1.0)[:, None, :]
    own_pos = parts[0] * query_count + jnp.arange(query_count)
    own_live = (own_pos[None, :] < own_dlen[:, None]).astype(F32).reshape(own_tokens, 1)
    part = width // n_z // 2

    def pair_sums(kept, arrived):
        shape = kept.shape[1:]
        return run(
            pair_sum_kernel,
            [kept, arrived],
            [shaped(shape, F32)] + [shaped(shape, BF16)] * (n_z - 1),
        )

    def sum_z(own, out, cols):
        arrived = [shift_z(block, i + 1) for i, block in enumerate(out)]
        return run(
            functools.partial(final_sum_kernel, cols),
            [own, *arrived],
            [shaped((own.shape[0], c), BF16) for c in cols],
        )

    to_plane = [
        ((h * 4 + 2 * a + b) * 4 + z, (b * 4 + z) * 4 + 2 * h + a)
        for h in range(2)
        for a in range(2)
        for b in range(2)
        for z in range(4)
    ]

    def gather_dp(block):
        pieces = [block, swap(block, "x")]
        pieces = pieces + [swap(p, "hi") for p in pieces]
        return [q for p in pieces for q in (p, swap(p, "core"))]

    def to_planes(rows):
        return lax.ppermute(rows, AXES, to_plane)

    def beside(cols, rows):
        return jnp.concatenate([cols, rows], 1)

    def both(cols, rows=part):
        return [shaped((n_z, rows, cols), BF16)] * 2

    def tokens_scratch(cols):
        return pltpu.VMEM((all_tokens, cols), BF16)


    heads = shaped((4, row_count, query_count, local), BF16)
    sent = shaped((all_tokens // 2, width), BF16)
    kept = shaped((all_tokens // 2, width), F32)
    own_f32 = shaped((own_tokens, width), F32)
    own_low = shaped((own_tokens, width), BF16)
    rstd_shape = shaped((own_tokens, 128), F32)
    sums_shape = shaped((8, width), F32)
    qkv, mixed_self, s, k = run(
        self_fwd_kernel,
        [*[after(t, mems[3]) for t in tokens], w_qkv, w_out, biases, self_mask],
        [shaped((4, row_count, query_count, 3 * local), BF16), heads, sent, kept],
    )
    n_one, rstd_one, one_low = run(
        norm_one_kernel,
        [*cross_links(s, k), own_in, out_bias[None], norm_gain, norm_bias],
        [own_f32, rstd_shape, own_low],
    )
    ones = gather_j(one_low)
    kv_shape = shaped((4 * slots, 2 * local), BF16)
    kv2 = run(memory_kv_kernel, [*mems, w_two, biases], [kv_shape] * row_count)
    query_two, mixed_cross, s, k = run(
        functools.partial(cross_fwd_kernel, row_count),
        [*ones, w_two, w_out2, biases, *kv2, q_code, k_code],
        [heads, heads, sent, kept],
    )
    n_two, rstd_two, two_low = run(
        norm_two_kernel,
        [*cross_links(s, k), n_one, biases, norm_gain, norm_bias],
        [own_f32, rstd_shape, own_low],
    )
    twos = gather_j(two_low)
    active, slope, s, k = run(
        ffn_fwd_kernel,
        [*twos, w_first, w_second, ffn_bias[None]],
        [shaped((all_tokens, ff_local), BF16), shaped((all_tokens, ff_local), F32), sent, kept],
    )
    mixed_out, d_three, own_f3, sums_three = run(
        norm_three_kernel,
        [*cross_links(s, k), n_two, biases, norm_gain, norm_bias, own_cot, own_live],
        [own_low, own_f32, own_low, sums_shape],
    )
    own_out = mixed_out.reshape(dec_in.shape)

    f3 = gather_j(own_f3)
    du, ff_sum, s, k = run(
        ffn_bwd_kernel,
        [*f3, w_first, w_second, slope],
        [shaped((all_tokens, ff_local), BF16), shaped((1, ff_local), F32), sent, kept],
    )
    k, arrived, crossed = cross_links(s, k)
    if fast:
        g_ffn = run(
            ffn_grad_kernel,
            [*twos, du, active, *f3],
            shaped((2, n_z, part, ff_local + width), BF16),
        )
        crossed = after(crossed, g_ffn)
        g_ffn = lax.psum_scatter(
            g_ffn.reshape(2 * n_z * part, -1), ("hi", "z"), scatter_dimension=0, tiled=True
        )
    d_two, own_f2, sums_two = run(
        functools.partial(norm_back_kernel, 1),
        [k, arrived, crossed, d_three, n_two, rstd_two, norm_gain],
        [own_f32, own_low, sums_shape],
    )
    f2 = gather_j(own_f2)
    dq2, *dkv2, cross_sums, s, k = run(
        functools.partial(cross_bwd_kernel, row_count),
        [*f2, w_two, w_out2, query_two, *kv2, q_code, k_code],
        [heads] + [kv_shape] * row_count + [shaped((8, local), F32), sent, kept],
        scratch=[pltpu.VMEM(heads.shape, BF16)],
    )
    d_one, own_f1, sums_one = run(
        functools.partial(norm_back_kernel, 0),
        [*cross_links(s, k), d_two, n_one, rstd_one, norm_gain],
        [own_f32, own_low, sums_shape],
    )
    f1 = gather_j(own_f1)
    dq2 = dq2.reshape(all_tokens, local)
    o2 = mixed_cross.reshape(all_tokens, local)
    if fast:
        kept_m, sent_m = run(
            functools.partial(memory_grad_kernel, n_z, row_count),
            mems + dkv2,
            both(2 * local),
            scratch=[pltpu.VMEM((4 * slots, width // 2), BF16)],
        )
        kept_b, sent_b = run(
            functools.partial(cross_grad_kernel, n_z),
            [*ones, dq2, kept_m, sent_m, o2, *f2],
            both(4 * local),
            scratch=[tokens_scratch(width // 2), tokens_scratch(width)],
        )
        f1 = [after(f, sent_b) for f in f1]
    dqkv, sum_qkv, s, k = run(
        self_bwd_kernel,
        [*f1, w_qkv, w_out, qkv, self_mask],
        [
            shaped((4, row_count, query_count, 3 * local), BF16),
            shaped((1, 3 * local), F32),
            sent,
            kept,
        ],
    )
    own_d = add_crossed(*cross_links(s, k), d_one)

    ff_rows = ff_width // width
    n_small = 16
    small = run(
        small_kernel,
        [sums_three, sums_two, sums_one, cross_sums, ff_sum],
        shaped((n_small, width), F32),
    )
    dqkv = dqkv.reshape(all_tokens, -1)
    o1 = mixed_self.reshape(all_tokens, local)
    half_slots = (2, row_count, slots, width)
    memory_outs = [shaped(half_slots, BF16), shaped(half_slots, F32)]
    if fast:
        arrived_b = swap(sent_b, "hi")
        kept_a, sent_a = run(
            functools.partial(self_grad_kernel, n_z),
            [*tokens, dqkv, sum_qkv, small, o1, *f1],
            both(4 * local, part + 16),
            scratch=[tokens_scratch(width // 2), tokens_scratch(width)],
        )
        sums_c = after(g_ffn, sent_a)
        arrived_a = swap(after(sent_a, arrived_b), "hi")
        own_b, *out_b = pair_sums(kept_b, after(arrived_b, sums_c))
        s_m, k_m = run(
            memory_back_kernel, [after(dkv, out_b[0]) for dkv in dkv2] + [w_two], memory_outs
        )
        links_m = cross_links(s_m, k_m)
        cols_b, rows_b = sum_z(own_b, out_b, (3 * local, local))
        own_a, *out_a = pair_sums(kept_a, after(arrived_a, rows_b, links_m[2]))
        pieces_c = gather_dp(after(sums_c, arrived_a))
        cols_a, rows_a = sum_z(own_a, out_a, (3 * local, local))
        planed = to_planes(beside(rows_b, rows_a[:part]))
        d_memory = add_crossed(*(t.reshape((-1, width)) for t in links_m))
        d_memory = after(d_memory, planed)
        block = run(
            join_kernel,
            [cols_b, cols_a, after(planed, d_memory), rows_a],
            shaped((part + 16, 8 * local), BF16),
        )
        mixed_out = transpose(after(own_out, planed))
        d_dec = transpose(after(own_d, planed).reshape(dec_in.shape))
        d_memory = transpose(after(d_memory, d_dec, mixed_out).reshape(memory.shape))
        g_first, g_second = run(
            ffn_out_kernel,
            pieces_c,
            [shaped((width // n_z, ff_width), F32), shaped((ff_width // n_z, width), F32)],
        )
        n_part = width // n_z
        g_proj, g_out, g_biases, g_out_bias, g_ffn_bias, g_norms = run(
            functools.partial(proj_out_kernel, n_z),
            gather_dp(block),
            [
                shaped((6, n_part, width), F32),
                shaped((2, n_part, width), F32),
                shaped((6, n_part), F32),
                shaped((1, n_part), F32),
                shaped((1, ff_width // n_z), F32),
                shaped((6, n_part), F32),
            ],
            scratch=[pltpu.VMEM((8, width), F32), pltpu.VMEM(small.shape, F32)],
        )
        g_out_bias, g_ffn_bias = g_out_bias[0], g_ffn_bias[0]
        g_gain, g_shift = g_norms[:3], g_norms[3:]
    else:
        mine = (jnp.arange(4) == j).astype(F32)[:, None]

        small = lax.psum(small, AXES)
        d_memory = add_crossed(
            *(
                t.reshape((-1, width))
                for t in cross_links(*run(memory_back_kernel, list(dkv2) + [w_two], memory_outs))
            )
        )

        d_memory = transpose(d_memory.reshape(memory.shape))
        d_dec = transpose(own_d.reshape(dec_in.shape))
        mixed_out = transpose(own_out)

        def col_grads(left, grads, n, parts=2):
            cols = grads.shape[1] // n * 4
            total = t_mm(left, grads).reshape(-1, n, parts, 1, cols // (4 * parts))
            full = (total * mine).reshape(-1, n, cols).transpose(1, 0, 2)
            out = lax.psum_scatter(full.astype(BF16), "z", scatter_dimension=1, tiled=True)
            return lax.psum(out.astype(F32), ("hi", "x", "core"))

        def row_grads(left, grads, parts=2):
            total = t_mm(left, grads).reshape(parts, 1, -1, width)
            full = (total * mine[:, :, None]).reshape(-1, width)
            out = lax.psum_scatter(full.astype(BF16), "z", scatter_dimension=0, tiled=True)
            return lax.psum(out.astype(F32), ("hi", "x", "core"))

        def joined(pieces):
            return jnp.concatenate(pieces, 0)

        g_first = col_grads(joined(twos), du, 1, 4)[0]
        g_second = row_grads(active, joined(f3), 4)
        g_qkv = col_grads(joined(tokens), dqkv, 3)
        g_q2 = col_grads(joined(ones), dq2, 1)
        rows_of = jnp.concatenate(mems, 1).reshape(-1, width)
        g_kv2 = col_grads(rows_of, joined(dkv2), 2)
        g_proj = jnp.concatenate([g_qkv, g_q2, g_kv2], 0)
        g_out = jnp.stack([row_grads(o1, joined(f1)), row_grads(o2, joined(f2))])
        sums_qkv = (sum_qkv.reshape(3, 2, 1, width // 8) * mine).reshape(3, width)
        sums_qkv = lax.psum(sums_qkv, AXES)

        n_part = width // n_z
        cut = lax.dynamic_slice_in_dim(small, zi * n_part, n_part, 1)
        cut_qkv = lax.dynamic_slice_in_dim(sums_qkv, zi * n_part, n_part, 1)
        g_biases = jnp.concatenate([cut_qkv[0:1], cut_qkv[2:3], cut[0:4]], 0)
        g_out_bias = cut[4]
        g_ffn_bias = lax.dynamic_slice_in_dim(
            small[5 : 5 + ff_rows].reshape(-1), zi * (ff_width // n_z), ff_width // n_z
        )
        g_gain = cut[5 + ff_rows : 8 + ff_rows]
        g_shift = cut[8 + ff_rows : 11 + ff_rows]
    d_dec = d_dec.astype(F32)
    return (
        mixed_out,
        d_dec,
        d_memory,
        g_proj,
        g_out,
        g_first,
        g_second,
        g_biases,
        g_out_bias,
        g_ffn_bias,
        g_gain,
        g_shift,
    )


def solution(mesh):
    devices = mesh.devices
    inner = Mesh(devices.reshape(devices.shape[0] // 4, 2, 2, devices.shape[1]), AXES)
    dp = ("hi", "x", "core")
    in_specs = (
        P(dp, "z", None),
        P(dp, None, "z", None),
        P(None, AXES, None),
        P(None, AXES, None),
        P(AXES, None),
        P(AXES, None),
        P(),
        P(),
        P(),
        P(),
        P(),
        P(),
        P(),
        P(dp, None, None),
        P(dp, None),
        P(dp, "z", None),
    )
    out_specs = (
        P(dp, "z", None),
        P(dp, "z", None),
        P(dp, None, "z", None),
        P(None, "z", None),
        P(None, "z", None),
        P("z", None),
        P("z", None),
        P(None, "z"),
        P("z"),
        P("z"),
        P(None, "z"),
        P(None, "z"),
    )
    return jax.shard_map(
        per_device, mesh=inner, in_specs=in_specs, out_specs=out_specs, check_vma=False
    )
```

profile of v0, /device:TPU:2, one launch (start us, length us, event | category | flops | bytes accessed | tf_op | source)
XLA Modules:
  0.0 545.4 jit_solution(16814222216168219907)
XLA Ops:
  7.2 3.5 collective-permute-start
  12.1 3.3 collective-permute-start.1
  15.4 4.7 collective-permute-done.1
  24.1 2.4 collective-permute-start.8
  27.9 9.4 %collective-permute-done.9.e2 = bf16[32,2560]{1,0:T(8,128)(2,1)S(1)} collective-permute-done((bf16[32,2560]{1,0:T(8,128)(2,1)}, bf16[32,2560]{1,0:T(8,128)(2,1)S(1)}, u32[]{:S(2)}, u32[]{:S(2)}) %collective-permute-start.9) | collective-permute-done | bytes 163872 | tf_op jit(solution)/shard_map/ppermute | solution.py:40
  37.3 3.6 collective-permute-done.10.e3
  43.7 26.0 %collective-permute-done.2 = bf16[3,7,32,1024]{3,2,1,0:T(8,128)(2,1)S(1)} collective-permute-done((bf16[3,7,32,1024]{3,2,1,0:T(8,128)(2,1)}, bf16[3,7,32,1024]{3,2,1,0:T(8,128)(2,1)S(1)}, u32[]{:S(2)}, u32[]{:S(2)}) %collective-permute-start.2) | collective-permute-done | bytes 1376288 | tf_op jit(solution)/shard_map/ppermute | solution.py:717
  71.8 31.8 %collective-permute-done.22.second = bf16[128,1024]{1,0:T(8,128)(2,1)S(1)} collective-permute-done((bf16[128,1024]{1,0:T(8,128)(2,1)S(1)}, bf16[128,1024]{1,0:T(8,128)(2,1)S(1)}, u32[]{:S(2)}, u32[]{:S(2)}) %collective-permute-start.22) | collective-permute-done | bytes 262176 | tf_op jit(solution)/shard_map/ppermute | solution.py:771
  107.8 6.7 %collective-permute-done.5.x1 = bf16[96,1024]{1,0:T(8,128)(2,1)S(1)} collective-permute-done((bf16[96,1024]{1,0:T(8,128)(2,1)S(1)}, bf16[96,1024]{1,0:T(8,128)(2,1)S(1)}, u32[]{:S(2)}, u32[]{:S(2)}) %collective-permute-start.5) | collective-permute-done | bytes 196640 | tf_op jit(solution)/shard_map/ppermute | solution.py:40
  116.7 26.1 %all-gather.5.cloned.1.call-done = bf16[32,32,2048]{2,1,0:T(8,128)(2,1)} async-done(((bf16[4,32,2048]{2,1,0:T(8,128)(2,1)}), bf16[32,32,2048]{2,1,0:T(8,128)(2,1)}) %all-gather.5.cloned.1.call-update) | async-done | bytes 4194320 | tf_op jit(solution)/shard_map/all_gather | solution.py:773
  142.8 4.3 place_kernel.1
  147.1 5.2 self_fwd_kernel.1
  156.8 5.6 %collective-permute-done.12.crossed = bf16[96,1024]{1,0:T(8,128)(2,1)S(1)} collective-permute-done((bf16[96,1024]{1,0:T(8,128)(2,1)S(1)}, bf16[96,1024]{1,0:T(8,128)(2,1)S(1)}, u32[]{:S(2)}, u32[]{:S(2)}) %collective-permute-start.12) | collective-permute-done | bytes 196640 | tf_op jit(solution)/shard_map/ppermute | solution.py:40
  163.1 2.5 norm_one_kernel.1
  166.9 5.2 collective-permute-done.13.refs_1_.h1
  172.0 7.1 %memory_kv_kernel.1 = (bf16[896,512]{1,0:T(8,128)(2,1)}, bf16[896,512]{1,0:T(8,128)(2,1)}, bf16[896,512]{1,0:T(8,128)(2,1)}) custom-call(bf16[3,224,1024]{2,1,0:T(8,128)(2,1)} %bitcast.53, bf16[3,224,1024]{2,1,0:T(8,128)(2,1)} %copy-done.10, bf16[3,224,1024]{2,1,0:T(8,128)(2,1)} %collective-permute-done.16.m2.refs_2_, ...), custom_call_target="tpu_custom_call" | custom-call | flops 7699999744 | tf_op jit(solution)/shard_map/memory_kv_kernel/pallas_call | solution.py:140
  180.0 8.0 %cross_fwd_kernel.1 = (bf16[4,3,32,256]{3,2,1,0:T(8,128)(2,1)}, bf16[4,3,32,256]{3,2,1,0:T(8,128)(2,1)}, bf16[192,1024]{1,0:T(8,128)(2,1)}, f32[192,1024]{1,0:T(8,128)}) custom-call(bf16[96,1024]{1,0:T(8,128)(2,1)} %get-tuple-element.137.refs_0_.h0, bf16[96,1024]{1,0:T(8,128)(2,1)} %copy-done.28, bf16[96,1024]{1,0:T(8,128)(2,1)} %copy-done.29, ...), custom_call_target="tpu_custom_call" | custom-call | flops 8800000000 | tf_op jit(solution)/shard_map/cross_fwd_kernel/pallas_call | solution.py:140
  191.8 6.6 %collective-permute-done.18.crossed = bf16[96,1024]{1,0:T(8,128)(2,1)S(1)} collective-permute-done((bf16[96,1024]{1,0:T(8,128)(2,1)S(1)}, bf16[96,1024]{1,0:T(8,128)(2,1)S(1)}, u32[]{:S(2)}, u32[]{:S(2)}) %collective-permute-start.18) | collective-permute-done | bytes 196640 | tf_op jit(solution)/shard_map/ppermute | solution.py:40
  199.1 2.5 norm_two_kernel.1
  202.2 6.1 %collective-permute-done.19.h1.a1 = bf16[96,1024]{1,0:T(8,128)(2,1)S(1)} collective-permute-done((bf16[96,1024]{1,0:T(8,128)(2,1)}, bf16[96,1024]{1,0:T(8,128)(2,1)S(1)}, u32[]{:S(2)}, u32[]{:S(2)}) %collective-permute-start.19) | collective-permute-done | bytes 196640 | tf_op jit(solution)/shard_map/ppermute | solution.py:40
  208.3 8.9 %all-gather.7.cloned.1.call-done = bf16[64,32,1024]{2,1,0:T(8,128)(2,1)} async-done(((bf16[8,32,1024]{2,1,0:T(8,128)(2,1)}), bf16[64,32,1024]{2,1,0:T(8,128)(2,1)}) %all-gather.7.cloned.1.call-update) | async-done | bytes 4194320 | tf_op jit(solution)/shard_map/all_gather | solution.py:783
  217.2 4.5 place_ffn_kernel.1
  222.4 6.2 %ffn_fwd_kernel.1 = (bf16[384,1024]{1,0:T(8,128)(2,1)}, f32[384,1024]{1,0:T(8,128)}, bf16[192,1024]{1,0:T(8,128)(2,1)}, f32[192,1024]{1,0:T(8,128)}) custom-call(bf16[96,1024]{1,0:T(8,128)(2,1)} %get-tuple-element.146.h0.a0, bf16[96,1024]{1,0:T(8,128)(2,1)} %copy-done.31, bf16[96,1024]{1,0:T(8,128)(2,1)} %copy-done.32, bf16[96,1024]{1,0:T(8,128)(2,1)} %copy-done.33, ...), custom_call_target="tpu_custom_call" | custom-call | flops 6600000000 | tf_op jit(solution)/shard_map/ffn_fwd_kernel/pallas_call | solution.py:140
  228.6 2.7 collective-permute-start.25
  233.5 7.9 %collective-permute-done.25 = bf16[3,32,1024]{2,1,0:T(8,128)(2,1)S(1)} collective-permute-done((bf16[3,32,1024]{2,1,0:T(8,128)(2,1)S(1)}, bf16[3,32,1024]{2,1,0:T(8,128)(2,1)S(1)}, u32[]{:S(2)}, u32[]{:S(2)}) %collective-permute-start.25) | collective-permute-done | bytes 196640 | tf_op jit(solution)/shard_map/ppermute | solution.py:717
  241.4 2.9 collective-permute-done.24.crossed
  245.0 2.9 norm_three_kernel.1
  248.0 6.9 %collective-permute-done.26.f1 = bf16[96,1024]{1,0:T(8,128)(2,1)S(1)} collective-permute-done((bf16[96,1024]{1,0:T(8,128)(2,1)}, bf16[96,1024]{1,0:T(8,128)(2,1)S(1)}, u32[]{:S(2)}, u32[]{:S(2)}) %collective-permute-start.26) | collective-permute-done | bytes 196640 | tf_op jit(solution)/shard_map/ppermute | solution.py:40
  257.0 6.2 %ffn_bwd_kernel.1 = (bf16[384,1024]{1,0:T(8,128)(2,1)}, f32[1,1024]{1,0:T(1,128)}, bf16[192,1024]{1,0:T(8,128)(2,1)}, f32[192,1024]{1,0:T(8,128)}) custom-call(bf16[96,1024]{1,0:T(8,128)(2,1)} %get-tuple-element.156.f0, bf16[96,1024]{1,0:T(8,128)(2,1)} %copy-done.41, bf16[96,1024]{1,0:T(8,128)(2,1)} %copy-done.42, bf16[96,1024]{1,0:T(8,128)(2,1)} %copy-done.44, ...), custom_call_target="tpu_custom_call" | custom-call | flops 6600000000 | tf_op jit(solution)/shard_map/ffn_bwd_kernel/pallas_call | solution.py:140
  263.3 6.3 %ffn_grad_kernel.1 = bf16[2,4,128,2048]{3,2,1,0:T(8,128)(2,1)} custom-call(bf16[96,1024]{1,0:T(8,128)(2,1)} %get-tuple-element.146.h0.a0, bf16[96,1024]{1,0:T(8,128)(2,1)} %copy-done.31, bf16[96,1024]{1,0:T(8,128)(2,1)} %copy-done.32, bf16[96,1024]{1,0:T(8,128)(2,1)} %copy-done.33, bf16[384,1024]{1,0:T(8,128)(2,1)} %get-tuple-element.160.du, ...), custom_call_target="tpu_custom_call" | custom-call | flops 6600000000 | tf_op jit(solution)/shard_map/ffn_grad_kernel/pallas_call | solution.py:140
  272.7 6.7 %collective-permute-done.30.crossed = bf16[96,1024]{1,0:T(8,128)(2,1)S(1)} collective-permute-done((bf16[96,1024]{1,0:T(8,128)(2,1)S(1)}, bf16[96,1024]{1,0:T(8,128)(2,1)S(1)}, u32[]{:S(2)}, u32[]{:S(2)}) %collective-permute-start.30) | collective-permute-done | bytes 196640 | tf_op jit(solution)/shard_map/ppermute | solution.py:40
  280.0 2.7 norm_back_kernel.2
  283.0 6.2 %collective-permute-done.31.refs_1_.f1 = bf16[96,1024]{1,0:T(8,128)(2,1)S(1)} collective-permute-done((bf16[96,1024]{1,0:T(8,128)(2,1)}, bf16[96,1024]{1,0:T(8,128)(2,1)S(1)}, u32[]{:S(2)}, u32[]{:S(2)}) %collective-permute-start.31) | collective-permute-done | bytes 196640 | tf_op jit(solution)/shard_map/ppermute | solution.py:40
  291.3 10.7 %cross_bwd_kernel.1 = (bf16[4,3,32,256]{3,2,1,0:T(8,128)(2,1)}, bf16[896,512]{1,0:T(8,128)(2,1)}, bf16[896,512]{1,0:T(8,128)(2,1)}, bf16[896,512]{1,0:T(8,128)(2...) custom-call(bf16[96,1024]{1,0:T(8,128)(2,1)} %get-tuple-element.165.refs_0_.f0, ...), custom_call_target="tpu_custom_call" | custom-call | flops 12099999744 | tf_op jit(solution)/shard_map/cross_bwd_kernel/pallas_call | solution.py:140
  305.5 6.7 %collective-permute-done.36.crossed = bf16[96,1024]{1,0:T(8,128)(2,1)S(1)} collective-permute-done((bf16[96,1024]{1,0:T(8,128)(2,1)S(1)}, bf16[96,1024]{1,0:T(8,128)(2,1)S(1)}, u32[]{:S(2)}, u32[]{:S(2)}) %collective-permute-start.36) | collective-permute-done | bytes 196640 | tf_op jit(solution)/shard_map/ppermute | solution.py:40
  312.9 2.7 norm_back_kernel.3
  315.9 8.8 %memory_grad_kernel.1 = (bf16[4,128,512]{2,1,0:T(8,128)(2,1)}, bf16[4,128,512]{2,1,0:T(8,128)(2,1)}) custom-call(bf16[3,224,1024]{2,1,0:T(8,128)(2,1)} %bitcast.54, bf16[3,224,1024]{2,1,0:T(8,128)(2,1)} %copy-done.10, bf16[3,224,1024]{2,1,0:T(8,128)(2,1)} %collective-permute-done.16.m2.refs_2_, bf16[3,224,1024]{2,1,0:T(8,128)(2,1)} %collective-permute-done.4.m3.refs_3_, ...), custom_call_target="tpu_custom_call" | custom-call | flops 9900000256 | tf_op jit(solution)/shard_map/memory_grad_kernel/pallas_call | solution.py:140
  325.3 4.2 cross_grad_kernel.1
  332.4 6.3 %self_bwd_kernel.1 = (bf16[4,3,32,768]{3,2,1,0:T(8,128)(2,1)}, f32[1,768]{1,0:T(1,128)}, bf16[192,1024]{1,0:T(8,128)(2,1)}, f32[192,1024]{1,0:T(8,128)}) custom-call(bf16[96,1024]{1,0:T(8,128)(2,1)} %get-tuple-element.181.f0, bf16[96,1024]{1,0:T(8,128)(2,1)} %copy-done.38, bf16[96,1024]{1,0:T(8,128)(2,1)} %copy-done.39, bf16[96,1024]{1,0:T(8,128)(2,1)} %copy-done.40, ...), custom_call_target="tpu_custom_call" | custom-call | flops 6600000000 | tf_op jit(solution)/shard_map/self_bwd_kernel/pallas_call | solution.py:140
  338.6 4.5 self_grad_kernel.1
  343.1 16.6 %reduce-scatter.2.cloned.1.call-done.refs_0_ = bf16[128,2048]{1,0:T(8,128)(2,1)} async-done(((bf16[1024,2048]{1,0:T(8,128)(2,1)}), bf16[128,2048]{1,0:T(8,128)(2,1)}) %reduce-scatter.2.cloned.1.call-update) | async-done | bytes 524304 | tf_op jit(solution)/shard_map/reduce_scatter | solution.py:928
  361.5 2.7 pair_sum_kernel.2
  364.2 8.2 %memory_back_kernel.1 = (bf16[2,3,224,1024]{3,2,1,0:T(8,128)(2,1)}, f32[2,3,224,1024]{3,2,1,0:T(8,128)}) custom-call(bf16[896,512]{1,0:T(8,128)(2,1)} %get-tuple-element.204.refs_4_.refs_0_, bf16[896,512]{1,0:T(8,128)(2,1)} %get-tuple-element.205.refs_5_.refs_1_, bf16[896,512]{1,0:T(8,128)(2,1)} %get-tuple-element.206.refs_6_.refs_2_, bf16[1024,768]{1,0:T(8,128)(2,1)} %bitcast.70), custom_call_target="tpu_custom_call" | custom-call | flops 8800000000 | tf_op jit(solution)/shard_map/memory_back_kernel/pallas_call | solution.py:140
  373.0 4.7 collective-permute-done.44
  377.7 3.6 add_convert_fusion.1
  385.3 15.8 %collective-permute-done.43.arrived = bf16[4,144,1024]{2,1,0:T(8,128)(2,1)} collective-permute-done((bf16[4,144,1024]{2,1,0:T(8,128)(2,1)}, bf16[4,144,1024]{2,1,0:T(8,128)(2,1)}, u32[]{:S(2)}, u32[]{:S(2)}) %collective-permute-start.43) | collective-permute-done | bytes 1179680 | tf_op jit(solution)/shard_map/ppermute | solution.py:40
  406.3 8.3 %collective-permute-done.45 = bf16[1,3,224,1024]{3,2,1,0:T(8,128)(2,1)S(1)} collective-permute-done((bf16[1,3,224,1024]{3,2,1,0:T(8,128)(2,1)}, bf16[1,3,224,1024]{3,2,1,0:T(8,128)(2,1)S(1)}, u32[]{:S(2)}, u32[]{:S(2)}) %collective-permute-start.45) | collective-permute-done | bytes 1376288 | tf_op jit(solution)/shard_map/ppermute | solution.py:40
  414.6 2.8 pair_sum_kernel.3
  418.8 2.3 collective-permute-start.48
  425.9 3.6 collective-permute-done.46.refs_0_
  429.5 10.3 %collective-permute-done.47.refs_1_ = bf16[144,1024]{1,0:T(8,128)(2,1)} collective-permute-done((bf16[144,1024]{1,0:T(8,128)(2,1)}, bf16[144,1024]{1,0:T(8,128)(2,1)}, u32[]{:S(2)}, u32[]{:S(2)}) %collective-permute-start.47) | collective-permute-done | bytes 294944 | tf_op jit(solution)/shard_map/ppermute | solution.py:720
  444.3 8.2 %collective-permute-start.49 = (bf16[128,512]{1,0:T(8,128)(2,1)S(1)}, bf16[128,512]{1,0:T(8,128)(2,1)S(1)}, u32[]{:S(2)}, u32[]{:S(2)}) collective-permute-start(bf16[128,512]{1,0:T(8,128)(2,1)S(1)} %pad_maximum_fusion), channel_id=1, source_target_pairs={{0,0},{1,4},{2,8},{3,12},{4,16},{5,20},{6,24},{7,28},{8,1},{9,5},{... | collective-permute-start | bytes 393224 | tf_op jit(solution)/shard_map/ppermute | solution.py:859
  452.5 3.6 add_convert_fusion
  456.5 4.8 collective-permute-start.50
  461.3 2.1 join_kernel.1.refs_0_
  466.0 5.7 %collective-permute-start.53 = (bf16[3,32,1024]{2,1,0:T(8,128)(2,1)S(1)}, bf16[3,32,1024]{2,1,0:T(8,128)(2,1)S(1)}, u32[]{:S(2)}, u32[]{:S(2)}) collective-permute-start(bf16[3,32,1024]{2,1,0:T(8,128)(2,1)S(1)} %bitcast.42), channel_id=1, source_target_pairs={{0,0},{1,8},{2,4},{3,12},{4,2},{5,10},{6,6},{7,14},{8,1},{9,9},{10... | collective-permute-start | bytes 589832 | tf_op jit(solution)/shard_map/ppermute | solution.py:717
  471.7 8.0 %collective-permute-done.53 = bf16[3,32,1024]{2,1,0:T(8,128)(2,1)S(1)} collective-permute-done((bf16[3,32,1024]{2,1,0:T(8,128)(2,1)S(1)}, bf16[3,32,1024]{2,1,0:T(8,128)(2,1)S(1)}, u32[]{:S(2)}, u32[]{:S(2)}) %collective-permute-start.53) | collective-permute-done | bytes 196640 | tf_op jit(solution)/shard_map/ppermute | solution.py:717
  481.7 2.9 collective-permute-start.58
  489.7 8.5 %collective-permute-done.58.refs_4_ = bf16[144,2048]{1,0:T(8,128)(2,1)} collective-permute-done((bf16[144,2048]{1,0:T(8,128)(2,1)}, bf16[144,2048]{1,0:T(8,128)(2,1)}, u32[]{:S(2)}, u32[]{:S(2)}) %collective-permute-start.58) | collective-permute-done | bytes 589856 | tf_op jit(solution)/shard_map/ppermute | solution.py:40
  498.2 2.9 collective-permute-start.59
  501.1 9.6 %collective-permute-done.60.refs_6_ = bf16[144,2048]{1,0:T(8,128)(2,1)} collective-permute-done((bf16[144,2048]{1,0:T(8,128)(2,1)S(1)}, bf16[144,2048]{1,0:T(8,128)(2,1)}, u32[]{:S(2)}, u32[]{:S(2)}) %collective-permute-start.60) | collective-permute-done | bytes 589856 | tf_op jit(solution)/shard_map/ppermute | solution.py:40
  511.7 6.1 %ffn_out_kernel.1 = (f32[256,4096]{1,0:T(8,128)}, f32[1024,1024]{1,0:T(8,128)}) custom-call(bf16[128,2048]{1,0:T(8,128)(2,1)} %reduce-scatter.2.cloned.1.call-done.refs_0_, bf16[128,2048]{1,0:T(8,128)(2,1)} %collective-permute-done.62.refs_1_, bf16[128,2048]{1,0:T(8,128)(2,1)} %collective-permute-done.63.refs_2_, bf16[128,2048]{1,0:T(8,128)(2,1)} %copy-done.13, ...), custom_call_target="tpu_custom_call" | custom-call | flops 6600000000 | tf_op jit(solution)/shard_map/ffn_out_kernel/pallas_call | solution.py:140
  518.6 10.9 %collective-permute-done.54 = bf16[3,7,32,1024]{3,2,1,0:T(8,128)(2,1)S(1)} collective-permute-done((bf16[3,7,32,1024]{3,2,1,0:T(8,128)(2,1)S(1)}, bf16[3,7,32,1024]{3,2,1,0:T(8,128)(2,1)S(1)}, u32[]{:S(2)}, u32[]{:S(2)}) %collective-permute-start.54) | collective-permute-done | bytes 1376288 | tf_op jit(solution)/shard_map/ppermute | solution.py:717
  529.5 6.0 %proj_out_kernel.1 = (f32[6,256,1024]{2,1,0:T(8,128)}, f32[2,256,1024]{2,1,0:T(8,128)}, f32[6,256]{1,0:T(8,128)}, f32[1,256]{1,0:T(1,128)}, f32[1,1024]{1,0:T(1,128)}, /*index=5*/f32[6,256]{1,0:T(8,128)}) custom-call(bf16[144,2048]{1,0:T(8,128)(2,1)} %join_kernel.1.refs_0_, bf16[144,2048]{1,0:T(8,128)(2,1)} %collective-permute-done.55.refs_1_, ...), custom_call_target="tpu_custom_call" | custom-call | flops 7699999744 | tf_op jit(solution)/shard_map/proj_out_kernel/pallas_call | solution.py:140
  (276 shorter events, 86.8 us)
Async XLA Ops:
  7.2 135.6 %all-gather.5.cloned.1.call-start = ((), (), s32[]{:S(2)}) async-start(), calls=%async_computation.2 | async-start | bytes 4718592 | tf_op jit(solution)/shard_map/all_gather | solution.py:773
  7.2 12.9 %collective-permute-start = (bf16[3,32,1024]{2,1,0:T(8,128)(2,1)}, bf16[3,32,1024]{2,1,0:T(8,128)(2,1)S(1)}, u32[]{:S(2)}, u32[]{:S(2)}) collective-permute-start(bf16[3,32,1024]{2,1,0:T(8,128)(2,1)} %param.16), channel_id=1, source_target_pairs={{0,0},{1,8},{2,4},{3,12},{4,2},{5,10},{6,6},{7,14},{8,1},{9,9},{10... | collective-permute-start | bytes 589832 | tf_op jit(solution)/shard_map/ppermute | solution.py:717
  12.1 8.0 %collective-permute-start.1 = (s32[3,1024]{1,0:T(4,128)S(1)}, s32[3,1024]{1,0:T(4,128)S(1)}, u32[]{:S(2)}, u32[]{:S(2)}) collective-permute-start(s32[3,1024]{1,0:T(4,128)S(1)} %pad_add_fusion), channel_id=1, source_target_pairs={{0,0},{1,8},{2,4},{3,12},{4,2},{5,10},{6,6},{7,14},{8,1},{9,9},{10... | collective-permute-start | bytes 36872 | tf_op jit(solution)/shard_map/ppermute | solution.py:717
  20.1 49.6 %collective-permute-start.2 = (bf16[3,7,32,1024]{3,2,1,0:T(8,128)(2,1)}, bf16[3,7,32,1024]{3,2,1,0:T(8,128)(2,1)S(1)}, u32[]{:S(2)}, u32[]{:S(2)}) collective-permute-start(bf16[3,7,32,1024]{3,2,1,0:T(8,128)(2,1)} %param.17), channel_id=1, source_target_pairs={{0,0},{1,8},{2,4},{3,12},{4,2},{5,10},{6,6},{7,14},{8,1},{9,9},{10... | collective-permute-start | bytes 4128776 | tf_op jit(solution)/shard_map/ppermute | solution.py:717
  24.1 3.8 collective-permute-start.8
  26.5 10.8 %collective-permute-start.9 = (bf16[32,2560]{1,0:T(8,128)(2,1)}, bf16[32,2560]{1,0:T(8,128)(2,1)S(1)}, u32[]{:S(2)}, u32[]{:S(2)}) collective-permute-start(bf16[32,2560]{1,0:T(8,128)(2,1)} %get-tuple-element.130), channel_id=1, source_target_pairs={{0,8},{8,0},{1,9},{9,1},{2,10},{10,2},{3,11},{11,3},{4,12},{12,4},... | collective-permute-start | bytes 491528 | tf_op jit(solution)/shard_map/ppermute | solution.py:40
  26.5 14.4 %collective-permute-start.10 = (bf16[32,2560]{1,0:T(8,128)(2,1)}, bf16[32,2560]{1,0:T(8,128)(2,1)S(1)}, u32[]{:S(2)}, u32[]{:S(2)}) collective-permute-start(bf16[32,2560]{1,0:T(8,128)(2,1)} %get-tuple-element.131), channel_id=1, source_target_pairs={{0,12},{4,8},{8,4},{12,0},{1,13},{5,9},{9,5},{13,1},{2,14},{6,10},... | collective-permute-start | bytes 491528 | tf_op jit(solution)/shard_map/ppermute | solution.py:763
  69.7 147.4 %all-gather.7.cloned.1.call-start = ((), (), s32[]{:S(2)}) async-start(), calls=%async_computation.3 | async-start | bytes 4718592 | tf_op jit(solution)/shard_map/all_gather | solution.py:783
  69.8 36.8 %collective-permute-start.3 = (bf16[3,224,1024]{2,1,0:T(8,128)(2,1)S(1)}, bf16[3,224,1024]{2,1,0:T(8,128)(2,1)S(1)}, u32[]{:S(2)}, u32[]{:S(2)}) collective-permute-start(bf16[3,224,1024]{2,1,0:T(8,128)(2,1)S(1)} %bitcast.51), channel_id=1, source_target_pairs={{0,8},{8,0},{1,9},{9,1},{2,10},{10,2},{3,11},{11,3},{4,12},{12,4},... | collective-permute-start | bytes 4128776 | tf_op jit(solution)/shard_map/ppermute | solution.py:40
  69.9 33.7 %collective-permute-start.22 = (bf16[128,1024]{1,0:T(8,128)(2,1)S(1)}, bf16[128,1024]{1,0:T(8,128)(2,1)S(1)}, u32[]{:S(2)}, u32[]{:S(2)}) collective-permute-start(bf16[128,1024]{1,0:T(8,128)(2,1)S(1)} %copy-done.16), channel_id=1, source_target_pairs={{0,0},{1,1},{2,4},{3,5},{4,8},{5,9},{6,12},{7,13},{8,2},{9,3},{10,... | collective-permute-start | bytes 786440 | tf_op jit(solution)/shard_map/ppermute | solution.py:771
  106.4 253.3 %reduce-scatter.2.cloned.1.call-start = ((), (), s32[]{:S(2)}) async-start(), calls=%async_computation.1 | async-start | bytes 4718592 | tf_op jit(solution)/shard_map/reduce_scatter | solution.py:928
  106.6 9.4 %collective-permute-start.4 = (bf16[3,224,1024]{2,1,0:T(8,128)(2,1)S(1)}, bf16[3,224,1024]{2,1,0:T(8,128)(2,1)}, u32[]{:S(2)}, u32[]{:S(2)}) collective-permute-start(bf16[3,224,1024]{2,1,0:T(8,128)(2,1)S(1)} %collective-permute-done.3.m1.refs_1_), channel_id=1, source_target_pairs={{0,4},{4,0},{1,5},{5,1},{2,6},{6,2},{3,7},{7,3},{8,12},{12,8},{9,1... | collective-permute-start | bytes 4128776 | tf_op jit(solution)/shard_map/ppermute | solution.py:40
  107.2 7.4 %collective-permute-start.5 = (bf16[96,1024]{1,0:T(8,128)(2,1)S(1)}, bf16[96,1024]{1,0:T(8,128)(2,1)S(1)}, u32[]{:S(2)}, u32[]{:S(2)}) collective-permute-start(bf16[96,1024]{1,0:T(8,128)(2,1)S(1)} %bitcast.55), channel_id=1, source_target_pairs={{0,8},{8,0},{1,9},{9,1},{2,10},{10,2},{3,11},{11,3},{4,12},{12,4},... | collective-permute-start | bytes 589832 | tf_op jit(solution)/shard_map/ppermute | solution.py:40
  107.3 9.3 %collective-permute-start.6 = (bf16[96,1024]{1,0:T(8,128)(2,1)S(1)}, bf16[96,1024]{1,0:T(8,128)(2,1)}, u32[]{:S(2)}, u32[]{:S(2)}) collective-permute-start(bf16[96,1024]{1,0:T(8,128)(2,1)S(1)} %bitcast.56), channel_id=1, source_target_pairs={{0,4},{4,0},{1,5},{5,1},{2,6},{6,2},{3,7},{7,3},{8,12},{12,8},{9,1... | collective-permute-start | bytes 589832 | tf_op jit(solution)/shard_map/ppermute | solution.py:40
  115.3 56.7 %collective-permute-start.16 = (bf16[3,224,1024]{2,1,0:T(8,128)(2,1)S(1)}, bf16[3,224,1024]{2,1,0:T(8,128)(2,1)}, u32[]{:S(2)}, u32[]{:S(2)}) collective-permute-start(bf16[3,224,1024]{2,1,0:T(8,128)(2,1)S(1)} %bitcast.52), channel_id=1, source_target_pairs={{0,4},{4,0},{1,5},{5,1},{2,6},{6,2},{3,7},{7,3},{8,12},{12,8},{9,1... | collective-permute-start | bytes 4128776 | tf_op jit(solution)/shard_map/ppermute | solution.py:40
  155.4 7.0 %collective-permute-start.12 = (bf16[96,1024]{1,0:T(8,128)(2,1)S(1)}, bf16[96,1024]{1,0:T(8,128)(2,1)S(1)}, u32[]{:S(2)}, u32[]{:S(2)}) collective-permute-start(bf16[96,1024]{1,0:T(8,128)(2,1)S(1)} %add_convert_fusion.8), channel_id=1, source_target_pairs={{0,8},{8,0},{1,9},{9,1},{2,10},{10,2},{3,11},{11,3},{4,12},{12,4},... | collective-permute-start | bytes 589832 | tf_op jit(solution)/shard_map/ppermute | solution.py:40
  165.6 6.4 %collective-permute-start.13 = (bf16[96,1024]{1,0:T(8,128)(2,1)}, bf16[96,1024]{1,0:T(8,128)(2,1)S(1)}, u32[]{:S(2)}, u32[]{:S(2)}) collective-permute-start(bf16[96,1024]{1,0:T(8,128)(2,1)} %get-tuple-element.137.refs_0_.h0), channel_id=1, source_target_pairs={{0,8},{8,0},{1,9},{9,1},{2,10},{10,2},{3,11},{11,3},{4,12},{12,4},... | collective-permute-start | bytes 589832 | tf_op jit(solution)/shard_map/ppermute | solution.py:40
  166.8 12.3 %collective-permute-start.14 = (bf16[96,1024]{1,0:T(8,128)(2,1)}, bf16[96,1024]{1,0:T(8,128)(2,1)S(1)}, u32[]{:S(2)}, u32[]{:S(2)}) collective-permute-start(bf16[96,1024]{1,0:T(8,128)(2,1)} %get-tuple-element.137.refs_0_.h0), channel_id=1, source_target_pairs={{0,4},{4,0},{1,5},{5,1},{2,6},{6,2},{3,7},{7,3},{8,12},{12,8},{9,1... | collective-permute-start | bytes 589832 | tf_op jit(solution)/shard_map/ppermute | solution.py:40
  172.0 7.2 %collective-permute-start.15 = (bf16[96,1024]{1,0:T(8,128)(2,1)S(1)}, bf16[96,1024]{1,0:T(8,128)(2,1)S(1)}, u32[]{:S(2)}, u32[]{:S(2)}) collective-permute-start(bf16[96,1024]{1,0:T(8,128)(2,1)S(1)} %collective-permute-done.13.refs_1_.h1), channel_id=1, source_target_pairs={{0,4},{4,0},{1,5},{5,1},{2,6},{6,2},{3,7},{7,3},{8,12},{12,8},{9,1... | collective-permute-start | bytes 589832 | tf_op jit(solution)/shard_map/ppermute | solution.py:40
  191.1 7.2 %collective-permute-start.18 = (bf16[96,1024]{1,0:T(8,128)(2,1)S(1)}, bf16[96,1024]{1,0:T(8,128)(2,1)S(1)}, u32[]{:S(2)}, u32[]{:S(2)}) collective-permute-start(bf16[96,1024]{1,0:T(8,128)(2,1)S(1)} %add_convert_fusion.7), channel_id=1, source_target_pairs={{0,8},{8,0},{1,9},{9,1},{2,10},{10,2},{3,11},{11,3},{4,12},{12,4},... | collective-permute-start | bytes 589832 | tf_op jit(solution)/shard_map/ppermute | solution.py:40
  201.6 6.7 %collective-permute-start.19 = (bf16[96,1024]{1,0:T(8,128)(2,1)}, bf16[96,1024]{1,0:T(8,128)(2,1)S(1)}, u32[]{:S(2)}, u32[]{:S(2)}) collective-permute-start(bf16[96,1024]{1,0:T(8,128)(2,1)} %get-tuple-element.146.h0.a0), channel_id=1, source_target_pairs={{0,8},{8,0},{1,9},{9,1},{2,10},{10,2},{3,11},{11,3},{4,12},{12,4},... | collective-permute-start | bytes 589832 | tf_op jit(solution)/shard_map/ppermute | solution.py:40
  202.2 19.5 %collective-permute-start.20 = (bf16[96,1024]{1,0:T(8,128)(2,1)}, bf16[96,1024]{1,0:T(8,128)(2,1)S(1)}, u32[]{:S(2)}, u32[]{:S(2)}) collective-permute-start(bf16[96,1024]{1,0:T(8,128)(2,1)} %get-tuple-element.146.h0.a0), channel_id=1, source_target_pairs={{0,4},{4,0},{1,5},{5,1},{2,6},{6,2},{3,7},{7,3},{8,12},{12,8},{9,1... | collective-permute-start | bytes 589832 | tf_op jit(solution)/shard_map/ppermute | solution.py:40
  208.3 13.3 %collective-permute-start.21 = (bf16[96,1024]{1,0:T(8,128)(2,1)S(1)}, bf16[96,1024]{1,0:T(8,128)(2,1)S(1)}, u32[]{:S(2)}, u32[]{:S(2)}) collective-permute-start(bf16[96,1024]{1,0:T(8,128)(2,1)S(1)} %collective-permute-done.19.h1.a1), channel_id=1, source_target_pairs={{0,4},{4,0},{1,5},{5,1},{2,6},{6,2},{3,7},{7,3},{8,12},{12,8},{9,1... | collective-permute-start | bytes 589832 | tf_op jit(solution)/shard_map/ppermute | solution.py:40
  228.6 2.8 collective-permute-start.23
  228.6 12.8 %collective-permute-start.25 = (bf16[3,32,1024]{2,1,0:T(8,128)(2,1)S(1)}, bf16[3,32,1024]{2,1,0:T(8,128)(2,1)S(1)}, u32[]{:S(2)}, u32[]{:S(2)}) collective-permute-start(bf16[3,32,1024]{2,1,0:T(8,128)(2,1)S(1)} %copy-done.24), channel_id=1, source_target_pairs={{0,0},{1,8},{2,4},{3,12},{4,2},{5,10},{6,6},{7,14},{8,1},{9,9},{10... | collective-permute-start | bytes 589832 | tf_op jit(solution)/shard_map/ppermute | solution.py:717
  232.6 11.7 %collective-permute-start.24 = (bf16[96,1024]{1,0:T(8,128)(2,1)S(1)}, bf16[96,1024]{1,0:T(8,128)(2,1)S(1)}, u32[]{:S(2)}, u32[]{:S(2)}) collective-permute-start(bf16[96,1024]{1,0:T(8,128)(2,1)S(1)} %add_convert_fusion.6), channel_id=1, source_target_pairs={{0,8},{8,0},{1,9},{9,1},{2,10},{10,2},{3,11},{11,3},{4,12},{12,4},... | collective-permute-start | bytes 589832 | tf_op jit(solution)/shard_map/ppermute | solution.py:40
  247.9 7.0 %collective-permute-start.26 = (bf16[96,1024]{1,0:T(8,128)(2,1)}, bf16[96,1024]{1,0:T(8,128)(2,1)S(1)}, u32[]{:S(2)}, u32[]{:S(2)}) collective-permute-start(bf16[96,1024]{1,0:T(8,128)(2,1)} %get-tuple-element.156.f0), channel_id=1, source_target_pairs={{0,8},{8,0},{1,9},{9,1},{2,10},{10,2},{3,11},{11,3},{4,12},{12,4},... | collective-permute-start | bytes 589832 | tf_op jit(solution)/shard_map/ppermute | solution.py:40
  247.9 7.0 %collective-permute-start.27 = (bf16[96,1024]{1,0:T(8,128)(2,1)}, bf16[96,1024]{1,0:T(8,128)(2,1)S(1)}, u32[]{:S(2)}, u32[]{:S(2)}) collective-permute-start(bf16[96,1024]{1,0:T(8,128)(2,1)} %get-tuple-element.156.f0), channel_id=1, source_target_pairs={{0,4},{4,0},{1,5},{5,1},{2,6},{6,2},{3,7},{7,3},{8,12},{12,8},{9,1... | collective-permute-start | bytes 589832 | tf_op jit(solution)/shard_map/ppermute | solution.py:40
  272.3 7.0 %collective-permute-start.30 = (bf16[96,1024]{1,0:T(8,128)(2,1)S(1)}, bf16[96,1024]{1,0:T(8,128)(2,1)S(1)}, u32[]{:S(2)}, u32[]{:S(2)}) collective-permute-start(bf16[96,1024]{1,0:T(8,128)(2,1)S(1)} %add_convert_fusion.5), channel_id=1, source_target_pairs={{0,8},{8,0},{1,9},{9,1},{2,10},{10,2},{3,11},{11,3},{4,12},{12,4},... | collective-permute-start | bytes 589832 | tf_op jit(solution)/shard_map/ppermute | solution.py:40
  282.7 6.4 %collective-permute-start.31 = (bf16[96,1024]{1,0:T(8,128)(2,1)}, bf16[96,1024]{1,0:T(8,128)(2,1)S(1)}, u32[]{:S(2)}, u32[]{:S(2)}) collective-permute-start(bf16[96,1024]{1,0:T(8,128)(2,1)} %get-tuple-element.165.refs_0_.f0), channel_id=1, source_target_pairs={{0,8},{8,0},{1,9},{9,1},{2,10},{10,2},{3,11},{11,3},{4,12},{12,4},... | collective-permute-start | bytes 589832 | tf_op jit(solution)/shard_map/ppermute | solution.py:40
  283.0 6.2 %collective-permute-start.32 = (bf16[96,1024]{1,0:T(8,128)(2,1)}, bf16[96,1024]{1,0:T(8,128)(2,1)S(1)}, u32[]{:S(2)}, u32[]{:S(2)}) collective-permute-start(bf16[96,1024]{1,0:T(8,128)(2,1)} %get-tuple-element.165.refs_0_.f0), channel_id=1, source_target_pairs={{0,4},{4,0},{1,5},{5,1},{2,6},{6,2},{3,7},{7,3},{8,12},{12,8},{9,1... | collective-permute-start | bytes 589832 | tf_op jit(solution)/shard_map/ppermute | solution.py:40
  305.0 7.2 %collective-permute-start.36 = (bf16[96,1024]{1,0:T(8,128)(2,1)S(1)}, bf16[96,1024]{1,0:T(8,128)(2,1)S(1)}, u32[]{:S(2)}, u32[]{:S(2)}) collective-permute-start(bf16[96,1024]{1,0:T(8,128)(2,1)S(1)} %add_convert_fusion.4), channel_id=1, source_target_pairs={{0,8},{8,0},{1,9},{9,1},{2,10},{10,2},{3,11},{11,3},{4,12},{12,4},... | collective-permute-start | bytes 589832 | tf_op jit(solution)/shard_map/ppermute | solution.py:40
  315.6 9.2 %collective-permute-start.37 = (bf16[96,1024]{1,0:T(8,128)(2,1)}, bf16[96,1024]{1,0:T(8,128)(2,1)S(1)}, u32[]{:S(2)}, u32[]{:S(2)}) collective-permute-start(bf16[96,1024]{1,0:T(8,128)(2,1)} %get-tuple-element.181.f0), channel_id=1, source_target_pairs={{0,8},{8,0},{1,9},{9,1},{2,10},{10,2},{3,11},{11,3},{4,12},{12,4},... | collective-permute-start | bytes 589832 | tf_op jit(solution)/shard_map/ppermute | solution.py:40
  324.8 6.8 %collective-permute-start.38 = (bf16[96,1024]{1,0:T(8,128)(2,1)S(1)}, bf16[96,1024]{1,0:T(8,128)(2,1)S(1)}, u32[]{:S(2)}, u32[]{:S(2)}) collective-permute-start(bf16[96,1024]{1,0:T(8,128)(2,1)S(1)} %copy-done.37), channel_id=1, source_target_pairs={{0,4},{4,0},{1,5},{5,1},{2,6},{6,2},{3,7},{7,3},{8,12},{12,8},{9,1... | collective-permute-start | bytes 589832 | tf_op jit(solution)/shard_map/ppermute | solution.py:40
  324.8 6.8 %collective-permute-start.39 = (bf16[96,1024]{1,0:T(8,128)(2,1)S(1)}, bf16[96,1024]{1,0:T(8,128)(2,1)S(1)}, u32[]{:S(2)}, u32[]{:S(2)}) collective-permute-start(bf16[96,1024]{1,0:T(8,128)(2,1)S(1)} %collective-permute-done.37.f1), channel_id=1, source_target_pairs={{0,4},{4,0},{1,5},{5,1},{2,6},{6,2},{3,7},{7,3},{8,12},{12,8},{9,1... | collective-permute-start | bytes 589832 | tf_op jit(solution)/shard_map/ppermute | solution.py:40
  329.5 31.1 %collective-permute-start.34 = (bf16[4,128,1024]{2,1,0:T(8,128)(2,1)}, bf16[4,128,1024]{2,1,0:T(8,128)(2,1)S(1)}, u32[]{:S(2)}, u32[]{:S(2)}) collective-permute-start(bf16[4,128,1024]{2,1,0:T(8,128)(2,1)} %get-tuple-element.175), channel_id=1, source_target_pairs={{0,16},{16,0},{1,17},{17,1},{2,18},{18,2},{3,19},{19,3},{4,20},{20... | collective-permute-start | bytes 3145736 | tf_op jit(solution)/shard_map/ppermute | solution.py:40
  372.4 5.3 collective-permute-start.44
  372.4 28.7 %collective-permute-start.43 = (bf16[4,144,1024]{2,1,0:T(8,128)(2,1)}, bf16[4,144,1024]{2,1,0:T(8,128)(2,1)}, u32[]{:S(2)}, u32[]{:S(2)}) collective-permute-start(bf16[4,144,1024]{2,1,0:T(8,128)(2,1)} %get-tuple-element.203), channel_id=1, source_target_pairs={{0,16},{16,0},{1,17},{17,1},{2,18},{18,2},{3,19},{19,3},{4,20},{20... | collective-permute-start | bytes 3538952 | tf_op jit(solution)/shard_map/ppermute | solution.py:40
  381.3 33.2 %collective-permute-start.45 = (bf16[1,3,224,1024]{3,2,1,0:T(8,128)(2,1)}, bf16[1,3,224,1024]{3,2,1,0:T(8,128)(2,1)S(1)}, u32[]{:S(2)}, u32[]{:S(2)}) collective-permute-start(bf16[1,3,224,1024]{3,2,1,0:T(8,128)(2,1)} %add_convert_fusion.1), channel_id=1, source_target_pairs={{0,8},{8,0},{1,9},{9,1},{2,10},{10,2},{3,11},{11,3},{4,12},{12,4},... | collective-permute-start | bytes 4128776 | tf_op jit(solution)/shard_map/ppermute | solution.py:40
  383.0 18.1 %collective-permute-start.41 = (bf16[128,1024]{1,0:T(8,128)(2,1)S(1)}, bf16[128,1024]{1,0:T(8,128)(2,1)S(1)}, u32[]{:S(2)}, u32[]{:S(2)}) collective-permute-start(bf16[128,1024]{1,0:T(8,128)(2,1)S(1)} %copy-done.19), channel_id=1, source_target_pairs={{0,2},{1,3},{2,0},{3,1},{4,6},{5,7},{6,4},{7,5},{8,10},{9,11},{10,... | collective-permute-start | bytes 786440 | tf_op jit(solution)/shard_map/ppermute | solution.py:720
  383.3 19.1 %collective-permute-start.42 = (bf16[128,1024]{1,0:T(8,128)(2,1)S(1)}, bf16[128,1024]{1,0:T(8,128)(2,1)S(1)}, u32[]{:S(2)}, u32[]{:S(2)}) collective-permute-start(bf16[128,1024]{1,0:T(8,128)(2,1)S(1)} %copy-done.18), channel_id=1, source_target_pairs={{0,3},{1,0},{2,1},{3,2},{4,7},{5,4},{6,5},{7,6},{8,11},{9,8},{10,9... | collective-permute-start | bytes 786440 | tf_op jit(solution)/shard_map/ppermute | solution.py:720
  384.8 18.7 %collective-permute-start.40 = (bf16[128,1024]{1,0:T(8,128)(2,1)S(1)}, bf16[128,1024]{1,0:T(8,128)(2,1)S(1)}, u32[]{:S(2)}, u32[]{:S(2)}) collective-permute-start(bf16[128,1024]{1,0:T(8,128)(2,1)S(1)} %copy-done.17), channel_id=1, source_target_pairs={{0,1},{1,2},{2,3},{3,0},{4,5},{5,6},{6,7},{7,4},{8,9},{9,10},{10,1... | collective-permute-start | bytes 786440 | tf_op jit(solution)/shard_map/ppermute | solution.py:720
  401.1 17.8 %collective-permute-start.51 = (bf16[192,1024]{1,0:T(8,128)(2,1)}, bf16[192,1024]{1,0:T(8,128)(2,1)}, u32[]{:S(2)}, u32[]{:S(2)}) collective-permute-start(bf16[192,1024]{1,0:T(8,128)(2,1)} %get-tuple-element.217), channel_id=1, source_target_pairs={{0,4},{4,0},{1,5},{5,1},{2,6},{6,2},{3,7},{7,3},{8,12},{12,8},{9,1... | collective-permute-start | bytes 1179656 | tf_op jit(solution)/shard_map/ppermute | solution.py:40
  401.1 21.9 %collective-permute-start.65 = (bf16[128,2048]{1,0:T(8,128)(2,1)}, bf16[128,2048]{1,0:T(8,128)(2,1)}, u32[]{:S(2)}, u32[]{:S(2)}) collective-permute-start(bf16[128,2048]{1,0:T(8,128)(2,1)} %reduce-scatter.2.cloned.1.call-done.refs_0_), channel_id=1, source_target_pairs={{0,16},{16,0},{1,17},{17,1},{2,18},{18,2},{3,19},{19,3},{4,20},{20... | collective-permute-start | bytes 1572872 | tf_op jit(solution)/shard_map/ppermute | solution.py:40
  402.4 23.5 %collective-permute-start.63 = (bf16[128,2048]{1,0:T(8,128)(2,1)}, bf16[128,2048]{1,0:T(8,128)(2,1)}, u32[]{:S(2)}, u32[]{:S(2)}) collective-permute-start(bf16[128,2048]{1,0:T(8,128)(2,1)} %reduce-scatter.2.cloned.1.call-done.refs_0_), channel_id=1, source_target_pairs={{0,8},{8,0},{1,9},{9,1},{2,10},{10,2},{3,11},{11,3},{4,12},{12,4},... | collective-permute-start | bytes 1572872 | tf_op jit(solution)/shard_map/ppermute | solution.py:40
  417.3 12.2 %collective-permute-start.46 = (bf16[144,1024]{1,0:T(8,128)(2,1)}, bf16[144,1024]{1,0:T(8,128)(2,1)}, u32[]{:S(2)}, u32[]{:S(2)}) collective-permute-start(bf16[144,1024]{1,0:T(8,128)(2,1)} %get-tuple-element.211), channel_id=1, source_target_pairs={{0,1},{1,2},{2,3},{3,0},{4,5},{5,6},{6,7},{7,4},{8,9},{9,10},{10,1... | collective-permute-start | bytes 884744 | tf_op jit(solution)/shard_map/ppermute | solution.py:720
  417.9 21.9 %collective-permute-start.47 = (bf16[144,1024]{1,0:T(8,128)(2,1)}, bf16[144,1024]{1,0:T(8,128)(2,1)}, u32[]{:S(2)}, u32[]{:S(2)}) collective-permute-start(bf16[144,1024]{1,0:T(8,128)(2,1)} %get-tuple-element.212), channel_id=1, source_target_pairs={{0,2},{1,3},{2,0},{3,1},{4,6},{5,7},{6,4},{7,5},{8,10},{9,11},{10,... | collective-permute-start | bytes 884744 | tf_op jit(solution)/shard_map/ppermute | solution.py:720
  418.8 21.6 %collective-permute-start.48 = (bf16[144,1024]{1,0:T(8,128)(2,1)}, bf16[144,1024]{1,0:T(8,128)(2,1)}, u32[]{:S(2)}, u32[]{:S(2)}) collective-permute-start(bf16[144,1024]{1,0:T(8,128)(2,1)} %get-tuple-element.213), channel_id=1, source_target_pairs={{0,3},{1,0},{2,1},{3,2},{4,7},{5,4},{6,5},{7,6},{8,11},{9,8},{10,9... | collective-permute-start | bytes 884744 | tf_op jit(solution)/shard_map/ppermute | solution.py:720
  422.9 40.5 %collective-permute-start.52 = (bf16[96,1024]{1,0:T(8,128)(2,1)}, bf16[96,1024]{1,0:T(8,128)(2,1)}, u32[]{:S(2)}, u32[]{:S(2)}) collective-permute-start(bf16[96,1024]{1,0:T(8,128)(2,1)} %add_convert_fusion.3), channel_id=1, source_target_pairs={{0,8},{8,0},{1,9},{9,1},{2,10},{10,2},{3,11},{11,3},{4,12},{12,4},... | collective-permute-start | bytes 589832 | tf_op jit(solution)/shard_map/ppermute | solution.py:40
  425.9 55.8 %collective-permute-start.62 = (bf16[128,2048]{1,0:T(8,128)(2,1)}, bf16[128,2048]{1,0:T(8,128)(2,1)}, u32[]{:S(2)}, u32[]{:S(2)}) collective-permute-start(bf16[128,2048]{1,0:T(8,128)(2,1)} %reduce-scatter.2.cloned.1.call-done.refs_0_), channel_id=1, source_target_pairs={{0,4},{4,0},{1,5},{5,1},{2,6},{6,2},{3,7},{7,3},{8,12},{12,8},{9,1... | collective-permute-start | bytes 1572872 | tf_op jit(solution)/shard_map/ppermute | solution.py:40
  429.5 56.0 %collective-permute-start.66 = (bf16[128,2048]{1,0:T(8,128)(2,1)}, bf16[128,2048]{1,0:T(8,128)(2,1)}, u32[]{:S(2)}, u32[]{:S(2)}) collective-permute-start(bf16[128,2048]{1,0:T(8,128)(2,1)} %collective-permute-done.65.refs_4_), channel_id=1, source_target_pairs={{0,4},{4,0},{1,5},{5,1},{2,6},{6,2},{3,7},{7,3},{8,12},{12,8},{9,1... | collective-permute-start | bytes 1572872 | tf_op jit(solution)/shard_map/ppermute | solution.py:40
  439.8 47.0 %collective-permute-start.67 = (bf16[128,2048]{1,0:T(8,128)(2,1)}, bf16[128,2048]{1,0:T(8,128)(2,1)}, u32[]{:S(2)}, u32[]{:S(2)}) collective-permute-start(bf16[128,2048]{1,0:T(8,128)(2,1)} %collective-permute-done.63.refs_2_), channel_id=1, source_target_pairs={{0,16},{16,0},{1,17},{17,1},{2,18},{18,2},{3,19},{19,3},{4,20},{20... | collective-permute-start | bytes 1572872 | tf_op jit(solution)/shard_map/ppermute | solution.py:40
  444.3 12.2 %collective-permute-start.49 = (bf16[128,512]{1,0:T(8,128)(2,1)S(1)}, bf16[128,512]{1,0:T(8,128)(2,1)S(1)}, u32[]{:S(2)}, u32[]{:S(2)}) collective-permute-start(bf16[128,512]{1,0:T(8,128)(2,1)S(1)} %pad_maximum_fusion), channel_id=1, source_target_pairs={{0,0},{1,4},{2,8},{3,12},{4,16},{5,20},{6,24},{7,28},{8,1},{9,5},{... | collective-permute-start | bytes 393224 | tf_op jit(solution)/shard_map/ppermute | solution.py:859
  456.5 9.5 %collective-permute-start.50 = (bf16[3,32,1024]{2,1,0:T(8,128)(2,1)}, bf16[3,32,1024]{2,1,0:T(8,128)(2,1)S(1)}, u32[]{:S(2)}, u32[]{:S(2)}) collective-permute-start(bf16[3,32,1024]{2,1,0:T(8,128)(2,1)} %bitcast.17), channel_id=1, source_target_pairs={{0,0},{1,8},{2,4},{3,12},{4,2},{5,10},{6,6},{7,14},{8,1},{9,9},{10... | collective-permute-start | bytes 589832 | tf_op jit(solution)/shard_map/ppermute | solution.py:717
  463.5 21.1 %collective-permute-start.56 = (bf16[144,2048]{1,0:T(8,128)(2,1)}, bf16[144,2048]{1,0:T(8,128)(2,1)S(1)}, u32[]{:S(2)}, u32[]{:S(2)}) collective-permute-start(bf16[144,2048]{1,0:T(8,128)(2,1)} %join_kernel.1.refs_0_), channel_id=1, source_target_pairs={{0,8},{8,0},{1,9},{9,1},{2,10},{10,2},{3,11},{11,3},{4,12},{12,4},... | collective-permute-start | bytes 1769480 | tf_op jit(solution)/shard_map/ppermute | solution.py:40
  466.0 13.7 %collective-permute-start.53 = (bf16[3,32,1024]{2,1,0:T(8,128)(2,1)S(1)}, bf16[3,32,1024]{2,1,0:T(8,128)(2,1)S(1)}, u32[]{:S(2)}, u32[]{:S(2)}) collective-permute-start(bf16[3,32,1024]{2,1,0:T(8,128)(2,1)S(1)} %bitcast.42), channel_id=1, source_target_pairs={{0,0},{1,8},{2,4},{3,12},{4,2},{5,10},{6,6},{7,14},{8,1},{9,9},{10... | collective-permute-start | bytes 589832 | tf_op jit(solution)/shard_map/ppermute | solution.py:717
  479.7 49.8 %collective-permute-start.54 = (bf16[3,7,32,1024]{3,2,1,0:T(8,128)(2,1)S(1)}, bf16[3,7,32,1024]{3,2,1,0:T(8,128)(2,1)S(1)}, u32[]{:S(2)}, u32[]{:S(2)}) collective-permute-start(bf16[3,7,32,1024]{3,2,1,0:T(8,128)(2,1)S(1)} %bitcast.41), channel_id=1, source_target_pairs={{0,0},{1,8},{2,4},{3,12},{4,2},{5,10},{6,6},{7,14},{8,1},{9,9},{10... | collective-permute-start | bytes 4128776 | tf_op jit(solution)/shard_map/ppermute | solution.py:717
  481.7 16.5 %collective-permute-start.58 = (bf16[144,2048]{1,0:T(8,128)(2,1)}, bf16[144,2048]{1,0:T(8,128)(2,1)}, u32[]{:S(2)}, u32[]{:S(2)}) collective-permute-start(bf16[144,2048]{1,0:T(8,128)(2,1)} %join_kernel.1.refs_0_), channel_id=1, source_target_pairs={{0,16},{16,0},{1,17},{17,1},{2,18},{18,2},{3,19},{19,3},{4,20},{20... | collective-permute-start | bytes 1769480 | tf_op jit(solution)/shard_map/ppermute | solution.py:40
  484.6 26.1 %collective-permute-start.60 = (bf16[144,2048]{1,0:T(8,128)(2,1)S(1)}, bf16[144,2048]{1,0:T(8,128)(2,1)}, u32[]{:S(2)}, u32[]{:S(2)}) collective-permute-start(bf16[144,2048]{1,0:T(8,128)(2,1)S(1)} %collective-permute-done.56.refs_2_), channel_id=1, source_target_pairs={{0,16},{16,0},{1,17},{17,1},{2,18},{18,2},{3,19},{19,3},{4,20},{20... | collective-permute-start | bytes 1769480 | tf_op jit(solution)/shard_map/ppermute | solution.py:40
  485.5 3.0 collective-permute-start.64
  488.6 40.9 %collective-permute-start.55 = (bf16[144,2048]{1,0:T(8,128)(2,1)}, bf16[144,2048]{1,0:T(8,128)(2,1)}, u32[]{:S(2)}, u32[]{:S(2)}) collective-permute-start(bf16[144,2048]{1,0:T(8,128)(2,1)} %join_kernel.1.refs_0_), channel_id=1, source_target_pairs={{0,4},{4,0},{1,5},{5,1},{2,6},{6,2},{3,7},{7,3},{8,12},{12,8},{9,1... | collective-permute-start | bytes 1769480 | tf_op jit(solution)/shard_map/ppermute | solution.py:40
  489.3 40.2 %collective-permute-start.57 = (bf16[144,2048]{1,0:T(8,128)(2,1)S(1)}, bf16[144,2048]{1,0:T(8,128)(2,1)}, u32[]{:S(2)}, u32[]{:S(2)}) collective-permute-start(bf16[144,2048]{1,0:T(8,128)(2,1)S(1)} %collective-permute-done.56.refs_2_), channel_id=1, source_target_pairs={{0,4},{4,0},{1,5},{5,1},{2,6},{6,2},{3,7},{7,3},{8,12},{12,8},{9,1... | collective-permute-start | bytes 1769480 | tf_op jit(solution)/shard_map/ppermute | solution.py:40
  498.2 31.3 %collective-permute-start.59 = (bf16[144,2048]{1,0:T(8,128)(2,1)}, bf16[144,2048]{1,0:T(8,128)(2,1)}, u32[]{:S(2)}, u32[]{:S(2)}) collective-permute-start(bf16[144,2048]{1,0:T(8,128)(2,1)} %collective-permute-done.58.refs_4_), channel_id=1, source_target_pairs={{0,4},{4,0},{1,5},{5,1},{2,6},{6,2},{3,7},{7,3},{8,12},{12,8},{9,1... | collective-permute-start | bytes 1769480 | tf_op jit(solution)/shard_map/ppermute | solution.py:40
  510.7 18.8 %collective-permute-start.61 = (bf16[144,2048]{1,0:T(8,128)(2,1)}, bf16[144,2048]{1,0:T(8,128)(2,1)}, u32[]{:S(2)}, u32[]{:S(2)}) collective-permute-start(bf16[144,2048]{1,0:T(8,128)(2,1)} %collective-permute-done.60.refs_6_), channel_id=1, source_target_pairs={{0,4},{4,0},{1,5},{5,1},{2,6},{6,2},{3,7},{7,3},{8,12},{12,8},{9,1... | collective-permute-start | bytes 1769480 | tf_op jit(solution)/shard_map/ppermute | solution.py:40
  (64 other events, 555.0 us)
Sparse Core Ops, SparseCore 0:
  69.8 72.8 all-gather.4
  145.4 71.6 all-gather.6
  269.7 89.9 reduce-scatter.1
where the time goes:
time: 556 us; the launch traced here: 545 us
  waiting for transfers between devices  290 us (52%)
  Pallas kernels  135 us (24%)
  starting transfers between devices  67.3 us (12%)
  other arithmetic  20.1 us (4%)
  local copies, waits for them, and re-layouts  18.4 us (3%)
  between operations  14.6 us (3%)
    pallas_call x30, Pallas kernels, run(): pl.pallas_call(kernel, name=base.__name__, in_specs=[anywhere if i in any...  135 us
    ppermute x53, waiting for transfers between devices, swap(): return lax.ppermute(values, axis, [(0, 1), (1, 0)])  129 us
    ppermute x7, waiting for transfers between devices, transpose(): return lax.ppermute(values, AXES, to_rows)  59 us
    ppermute x1, waiting for transfers between devices, per_device(): second = lax.ppermute(after(ffn_out, own_memory), AXES, to_quarter)  31.8 us
    all_gather x1, waiting for transfers between devices, per_device(): all_ab = lax.all_gather(after(buf_ab, own_memory), ('hi', 'z'), axis=0)  26.1 us
    ppermute x53, starting transfers between devices, swap(): return lax.ppermute(values, axis, [(0, 1), (1, 0)])  25.7 us
    ppermute x7, starting transfers between devices, transpose(): return lax.ppermute(values, AXES, to_rows)  23.9 us
    reduce_scatter x1, waiting for transfers between devices, per_device(): lax.psum_scatter(g_ffn.reshape(2 * n_z * part, -1), ('hi', 'z'), scatter_...  16.6 us
  transfers between devices with their start and end apart: 72, of which 42 were waited for; matrix products, arithmetic and copies ran while one was open for 4% of the time, Pallas kernels for 18%

commit v1 on v0

--- a/solution.py
+++ b/solution.py
@@ -753,7 +753,9 @@
     segs = transpose(jnp.concatenate([mem_seg.reshape(row_count, -1), dec_seg], 1))
     own_in = transpose(dec_in).reshape(own_tokens, width)
     tokens = gather_j(own_in)
-    own_memory = transpose(after(memory, own_in, segs)).reshape(row_count, slots, width)
+    first_rows = transpose(after(memory[:-1], own_in, segs))
+    last_row = transpose(after(memory[-1:], own_in, segs))
+    own_memory = jnp.concatenate([first_rows, last_row]).reshape(row_count, slots, width)
     mems = gather_j(own_memory)
     if fast:
         rows = proj_w.shape[1]
@@ -770,7 +772,7 @@
         buf_ab = run(pack_kernel, e + [out_w], shaped((4, rows, 2 * width), BF16))
         second = lax.ppermute(after(ffn_out, own_memory), AXES, to_quarter)
         buf_c = run(pack_ffn_kernel, e + [second], shaped((8, rows, ff_local), BF16))
-        all_ab = lax.all_gather(after(buf_ab, own_memory), ("hi", "z"), axis=0)
+        all_ab = lax.all_gather(after(buf_ab, first_rows), ("hi", "z"), axis=0)
         col_shape = shaped((2, 4, n_z, rows, 3 * local), BF16)
         row_shape = shaped((2, n_z, rows, width), BF16)
         placed = run(

time: 556 us -> 558 us (level)
    ppermute x1, waiting for transfers between devices: 31.8 us -> 10.2 us  [per_device(): second = lax.ppermute(after(ffn_out, own_memory), AXES, to_quarter)]
    all_gather x1, waiting for transfers between devices: 26.1 us -> 11 us  [per_device(): all_ab = lax.all_gather(after(buf_ab, first_rows), ('hi', 'z'), axis=0)]
    ppermute x1, waiting for transfers between devices: 3.63 us -> 17.9 us  [per_device(): lax.ppermute(e[3], ('x', 'core'), diag)]
    ppermute x7 -> x8, waiting for transfers between devices: 59 us -> 69.3 us  [transpose(): return lax.ppermute(values, AXES, to_rows)]
    ppermute x53, waiting for transfers between devices: 129 us -> 138 us  [swap(): return lax.ppermute(values, axis, [(0, 1), (1, 0)])]
    ppermute x7 -> x8, starting transfers between devices: 23.9 us -> 25.8 us  [transpose(): return lax.ppermute(values, AXES, to_rows)]
  transfers between devices with their start and end apart: 72 -> 73, of which waited for: 42 -> 43; matrix products, arithmetic and copies ran while one was open for 4% -> 5% of each run, Pallas kernels for 18% -> 18%
where the time goes in v1:
time: 558 us; the launch traced here: 547 us
  waiting for transfers between devices  287 us (51%)
  Pallas kernels  136 us (24%)
  starting transfers between devices  69.2 us (12%)
  other arithmetic  20.2 us (4%)
  local copies, waits for them, and re-layouts  20.1 us (4%)
  between operations  14.6 us (3%)
    ppermute x53, waiting for transfers between devices, swap(): return lax.ppermute(values, axis, [(0, 1), (1, 0)])  138 us
    pallas_call x30, Pallas kernels, run(): pl.pallas_call(kernel, name=base.__name__, in_specs=[anywhere if i in any...  136 us
    ppermute x8, waiting for transfers between devices, transpose(): return lax.ppermute(values, AXES, to_rows)  69.3 us
    ppermute x8, starting transfers between devices, transpose(): return lax.ppermute(values, AXES, to_rows)  25.8 us
    ppermute x53, starting transfers between devices, swap(): return lax.ppermute(values, axis, [(0, 1), (1, 0)])  25.7 us
    ppermute x1, waiting for transfers between devices, per_device(): lax.ppermute(e[3], ('x', 'core'), diag)  17.9 us
    reduce_scatter x1, waiting for transfers between devices, per_device(): lax.psum_scatter(g_ffn.reshape(2 * n_z * part, -1), ('hi', 'z'), scatter_...  16.5 us
    ppermute x6, waiting for transfers between devices, shift_z(): return lax.ppermute(values, 'z', [(i, (i + k) % n_z) for i in range(n_z)])  14.5 us
  transfers between devices with their start and end apart: 73, of which 43 were waited for; matrix products, arithmetic and copies ran while one was open for 5% of the time, Pallas kernels for 18%

profile of v1, /device:TPU:2, one launch (start us, length us, event | category | flops | bytes accessed | tf_op | source)
XLA Modules:
  0.0 546.7 jit_solution(17308555098324714687)
XLA Ops:
  7.2 3.5 collective-permute-start
  12.1 3.3 collective-permute-start.1
  16.6 3.5 collective-permute-done.1
  24.1 2.4 collective-permute-start.9
  27.9 9.4 %collective-permute-done.10.e2 = bf16[32,2560]{1,0:T(8,128)(2,1)S(1)} collective-permute-done((bf16[32,2560]{1,0:T(8,128)(2,1)}, bf16[32,2560]{1,0:T(8,128)(2,1)S(1)}, u32[]{:S(2)}, u32[]{:S(2)}) %collective-permute-start.10) | collective-permute-done | bytes 163872 | tf_op jit(solution)/shard_map/ppermute | solution.py:40
  37.3 17.9 %collective-permute-done.11.e3 = bf16[32,2560]{1,0:T(8,128)(2,1)S(1)} collective-permute-done((bf16[32,2560]{1,0:T(8,128)(2,1)}, bf16[32,2560]{1,0:T(8,128)(2,1)S(1)}, u32[]{:S(2)}, u32[]{:S(2)}) %collective-permute-start.11) | collective-permute-done | bytes 163872 | tf_op jit(solution)/shard_map/ppermute | solution.py:765
  61.0 37.6 %collective-permute-done.3 = bf16[1,7,32,1024]{3,2,1,0:T(8,128)(2,1)S(1)} collective-permute-done((bf16[1,7,32,1024]{3,2,1,0:T(8,128)(2,1)S(1)}, bf16[1,7,32,1024]{3,2,1,0:T(8,128)(2,1)S(1)}, u32[]{:S(2)}, u32[]{:S(2)}) %collective-permute-start.3) | collective-permute-done | bytes 458784 | tf_op jit(solution)/shard_map/ppermute | solution.py:717
  100.7 10.2 %collective-permute-done.23.second = bf16[128,1024]{1,0:T(8,128)(2,1)S(1)} collective-permute-done((bf16[128,1024]{1,0:T(8,128)(2,1)S(1)}, bf16[128,1024]{1,0:T(8,128)(2,1)S(1)}, u32[]{:S(2)}, u32[]{:S(2)}) %collective-permute-start.23) | collective-permute-done | bytes 262176 | tf_op jit(solution)/shard_map/ppermute | solution.py:773
  113.9 9.0 %collective-permute-done.4.m1.refs_1_ = bf16[3,224,1024]{2,1,0:T(8,128)(2,1)} collective-permute-done((bf16[3,224,1024]{2,1,0:T(8,128)(2,1)S(1)}, bf16[3,224,1024]{2,1,0:T(8,128)(2,1)}, u32[]{:S(2)}, u32[]{:S(2)}) %collective-permute-start.4) | collective-permute-done | bytes 1376288 | tf_op jit(solution)/shard_map/ppermute | solution.py:40
  124.0 6.7 %collective-permute-done.6.x1 = bf16[96,1024]{1,0:T(8,128)(2,1)S(1)} collective-permute-done((bf16[96,1024]{1,0:T(8,128)(2,1)S(1)}, bf16[96,1024]{1,0:T(8,128)(2,1)S(1)}, u32[]{:S(2)}, u32[]{:S(2)}) %collective-permute-start.6) | collective-permute-done | bytes 196640 | tf_op jit(solution)/shard_map/ppermute | solution.py:40
  132.2 11.0 %all-gather.5.cloned.1.call-done = bf16[32,32,2048]{2,1,0:T(8,128)(2,1)} async-done(((bf16[4,32,2048]{2,1,0:T(8,128)(2,1)}), bf16[32,32,2048]{2,1,0:T(8,128)(2,1)}) %all-gather.5.cloned.1.call-update) | async-done | bytes 4194320 | tf_op jit(solution)/shard_map/all_gather | solution.py:775
  143.2 4.3 place_kernel.1
  147.5 5.2 self_fwd_kernel.1
  157.3 5.6 %collective-permute-done.13.crossed = bf16[96,1024]{1,0:T(8,128)(2,1)S(1)} collective-permute-done((bf16[96,1024]{1,0:T(8,128)(2,1)S(1)}, bf16[96,1024]{1,0:T(8,128)(2,1)S(1)}, u32[]{:S(2)}, u32[]{:S(2)}) %collective-permute-start.13) | collective-permute-done | bytes 196640 | tf_op jit(solution)/shard_map/ppermute | solution.py:40
  163.6 2.5 norm_one_kernel.1
  167.3 5.2 collective-permute-done.14.refs_1_.h1
  172.5 7.2 %memory_kv_kernel.1 = (bf16[896,512]{1,0:T(8,128)(2,1)}, bf16[896,512]{1,0:T(8,128)(2,1)}, bf16[896,512]{1,0:T(8,128)(2,1)}) custom-call(bf16[3,224,1024]{2,1,0:T(8,128)(2,1)} %bitcast.43, bf16[3,224,1024]{2,1,0:T(8,128)(2,1)} %collective-permute-done.4.m1.refs_1_, bf16[3,224,1024]{2,1,0:T(8,128)(2,1)} %collective-permute-done.17.m2.refs_2_, ...), custom_call_target="tpu_custom_call" | custom-call | flops 7699999744 | tf_op jit(solution)/shard_map/memory_kv_kernel/pallas_call | solution.py:140
  180.4 8.0 %cross_fwd_kernel.1 = (bf16[4,3,32,256]{3,2,1,0:T(8,128)(2,1)}, bf16[4,3,32,256]{3,2,1,0:T(8,128)(2,1)}, bf16[192,1024]{1,0:T(8,128)(2,1)}, f32[192,1024]{1,0:T(8,128)}) custom-call(bf16[96,1024]{1,0:T(8,128)(2,1)} %get-tuple-element.139.refs_0_.h0, bf16[96,1024]{1,0:T(8,128)(2,1)} %copy-done.28, bf16[96,1024]{1,0:T(8,128)(2,1)} %copy-done.29, ...), custom_call_target="tpu_custom_call" | custom-call | flops 8800000000 | tf_op jit(solution)/shard_map/cross_fwd_kernel/pallas_call | solution.py:140
  192.3 6.6 %collective-permute-done.19.crossed = bf16[96,1024]{1,0:T(8,128)(2,1)S(1)} collective-permute-done((bf16[96,1024]{1,0:T(8,128)(2,1)S(1)}, bf16[96,1024]{1,0:T(8,128)(2,1)S(1)}, u32[]{:S(2)}, u32[]{:S(2)}) %collective-permute-start.19) | collective-permute-done | bytes 196640 | tf_op jit(solution)/shard_map/ppermute | solution.py:40
  199.6 2.6 norm_two_kernel.1
  202.7 6.1 %collective-permute-done.20.h1.a1 = bf16[96,1024]{1,0:T(8,128)(2,1)S(1)} collective-permute-done((bf16[96,1024]{1,0:T(8,128)(2,1)}, bf16[96,1024]{1,0:T(8,128)(2,1)S(1)}, u32[]{:S(2)}, u32[]{:S(2)}) %collective-permute-start.20) | collective-permute-done | bytes 196640 | tf_op jit(solution)/shard_map/ppermute | solution.py:40
  208.8 9.6 %all-gather.7.cloned.1.call-done = bf16[64,32,1024]{2,1,0:T(8,128)(2,1)} async-done(((bf16[8,32,1024]{2,1,0:T(8,128)(2,1)}), bf16[64,32,1024]{2,1,0:T(8,128)(2,1)}) %all-gather.7.cloned.1.call-update) | async-done | bytes 4194320 | tf_op jit(solution)/shard_map/all_gather | solution.py:785
  218.4 4.5 place_ffn_kernel.1
  223.7 6.3 %ffn_fwd_kernel.1 = (bf16[384,1024]{1,0:T(8,128)(2,1)}, f32[384,1024]{1,0:T(8,128)}, bf16[192,1024]{1,0:T(8,128)(2,1)}, f32[192,1024]{1,0:T(8,128)}) custom-call(bf16[96,1024]{1,0:T(8,128)(2,1)} %get-tuple-element.148.h0.a0, bf16[96,1024]{1,0:T(8,128)(2,1)} %copy-done.31, bf16[96,1024]{1,0:T(8,128)(2,1)} %copy-done.32, bf16[96,1024]{1,0:T(8,128)(2,1)} %copy-done.33, ...), custom_call_target="tpu_custom_call" | custom-call | flops 6600000000 | tf_op jit(solution)/shard_map/ffn_fwd_kernel/pallas_call | solution.py:140
  230.0 2.7 collective-permute-start.26
  234.8 8.0 %collective-permute-done.26 = bf16[3,32,1024]{2,1,0:T(8,128)(2,1)S(1)} collective-permute-done((bf16[3,32,1024]{2,1,0:T(8,128)(2,1)S(1)}, bf16[3,32,1024]{2,1,0:T(8,128)(2,1)S(1)}, u32[]{:S(2)}, u32[]{:S(2)}) %collective-permute-start.26) | collective-permute-done | bytes 196640 | tf_op jit(solution)/shard_map/ppermute | solution.py:717
  242.7 2.9 collective-permute-done.25.crossed
  246.3 2.9 norm_three_kernel.1
  249.3 6.9 %collective-permute-done.27.f1 = bf16[96,1024]{1,0:T(8,128)(2,1)S(1)} collective-permute-done((bf16[96,1024]{1,0:T(8,128)(2,1)}, bf16[96,1024]{1,0:T(8,128)(2,1)S(1)}, u32[]{:S(2)}, u32[]{:S(2)}) %collective-permute-start.27) | collective-permute-done | bytes 196640 | tf_op jit(solution)/shard_map/ppermute | solution.py:40
  258.4 6.2 %ffn_bwd_kernel.1 = (bf16[384,1024]{1,0:T(8,128)(2,1)}, f32[1,1024]{1,0:T(1,128)}, bf16[192,1024]{1,0:T(8,128)(2,1)}, f32[192,1024]{1,0:T(8,128)}) custom-call(bf16[96,1024]{1,0:T(8,128)(2,1)} %get-tuple-element.158.f0, bf16[96,1024]{1,0:T(8,128)(2,1)} %copy-done.41, bf16[96,1024]{1,0:T(8,128)(2,1)} %copy-done.42, bf16[96,1024]{1,0:T(8,128)(2,1)} %copy-done.44, ...), custom_call_target="tpu_custom_call" | custom-call | flops 6600000000 | tf_op jit(solution)/shard_map/ffn_bwd_kernel/pallas_call | solution.py:140
  264.6 6.3 %ffn_grad_kernel.1 = bf16[2,4,128,2048]{3,2,1,0:T(8,128)(2,1)} custom-call(bf16[96,1024]{1,0:T(8,128)(2,1)} %get-tuple-element.148.h0.a0, bf16[96,1024]{1,0:T(8,128)(2,1)} %copy-done.31, bf16[96,1024]{1,0:T(8,128)(2,1)} %copy-done.32, bf16[96,1024]{1,0:T(8,128)(2,1)} %copy-done.33, bf16[384,1024]{1,0:T(8,128)(2,1)} %get-tuple-element.162.du, ...), custom_call_target="tpu_custom_call" | custom-call | flops 6600000000 | tf_op jit(solution)/shard_map/ffn_grad_kernel/pallas_call | solution.py:140
  274.0 6.7 %collective-permute-done.31.crossed = bf16[96,1024]{1,0:T(8,128)(2,1)S(1)} collective-permute-done((bf16[96,1024]{1,0:T(8,128)(2,1)S(1)}, bf16[96,1024]{1,0:T(8,128)(2,1)S(1)}, u32[]{:S(2)}, u32[]{:S(2)}) %collective-permute-start.31) | collective-permute-done | bytes 196640 | tf_op jit(solution)/shard_map/ppermute | solution.py:40
  281.3 2.7 norm_back_kernel.2
  284.3 6.2 %collective-permute-done.32.refs_1_.f1 = bf16[96,1024]{1,0:T(8,128)(2,1)S(1)} collective-permute-done((bf16[96,1024]{1,0:T(8,128)(2,1)}, bf16[96,1024]{1,0:T(8,128)(2,1)S(1)}, u32[]{:S(2)}, u32[]{:S(2)}) %collective-permute-start.32) | collective-permute-done | bytes 196640 | tf_op jit(solution)/shard_map/ppermute | solution.py:40
  292.6 10.6 %cross_bwd_kernel.1 = (bf16[4,3,32,256]{3,2,1,0:T(8,128)(2,1)}, bf16[896,512]{1,0:T(8,128)(2,1)}, bf16[896,512]{1,0:T(8,128)(2,1)}, bf16[896,512]{1,0:T(8,128)(2...) custom-call(bf16[96,1024]{1,0:T(8,128)(2,1)} %get-tuple-element.167.refs_0_.f0, ...), custom_call_target="tpu_custom_call" | custom-call | flops 12099999744 | tf_op jit(solution)/shard_map/cross_bwd_kernel/pallas_call | solution.py:140
  306.8 6.7 %collective-permute-done.37.crossed = bf16[96,1024]{1,0:T(8,128)(2,1)S(1)} collective-permute-done((bf16[96,1024]{1,0:T(8,128)(2,1)S(1)}, bf16[96,1024]{1,0:T(8,128)(2,1)S(1)}, u32[]{:S(2)}, u32[]{:S(2)}) %collective-permute-start.37) | collective-permute-done | bytes 196640 | tf_op jit(solution)/shard_map/ppermute | solution.py:40
  314.2 2.7 norm_back_kernel.3
  317.3 8.9 %memory_grad_kernel.1 = (bf16[4,128,512]{2,1,0:T(8,128)(2,1)}, bf16[4,128,512]{2,1,0:T(8,128)(2,1)}) custom-call(bf16[3,224,1024]{2,1,0:T(8,128)(2,1)} %bitcast.44, bf16[3,224,1024]{2,1,0:T(8,128)(2,1)} %collective-permute-done.4.m1.refs_1_, bf16[3,224,1024]{2,1,0:T(8,128)(2,1)} %collective-permute-done.17.m2.refs_2_, ...), custom_call_target="tpu_custom_call" | custom-call | flops 9900000256 | tf_op jit(solution)/shard_map/memory_grad_kernel/pallas_call | solution.py:140
  326.6 4.2 cross_grad_kernel.1
  333.7 6.3 %self_bwd_kernel.1 = (bf16[4,3,32,768]{3,2,1,0:T(8,128)(2,1)}, f32[1,768]{1,0:T(1,128)}, bf16[192,1024]{1,0:T(8,128)(2,1)}, f32[192,1024]{1,0:T(8,128)}) custom-call(bf16[96,1024]{1,0:T(8,128)(2,1)} %get-tuple-element.183.f0, bf16[96,1024]{1,0:T(8,128)(2,1)} %copy-done.38, bf16[96,1024]{1,0:T(8,128)(2,1)} %copy-done.39, bf16[96,1024]{1,0:T(8,128)(2,1)} %copy-done.40, ...), custom_call_target="tpu_custom_call" | custom-call | flops 6600000000 | tf_op jit(solution)/shard_map/self_bwd_kernel/pallas_call | solution.py:140
  340.0 4.5 self_grad_kernel.1
  344.5 16.5 %reduce-scatter.2.cloned.1.call-done.refs_0_ = bf16[128,2048]{1,0:T(8,128)(2,1)} async-done(((bf16[1024,2048]{1,0:T(8,128)(2,1)}), bf16[128,2048]{1,0:T(8,128)(2,1)}) %reduce-scatter.2.cloned.1.call-update) | async-done | bytes 524304 | tf_op jit(solution)/shard_map/reduce_scatter | solution.py:930
  362.8 2.7 pair_sum_kernel.2
  365.5 8.2 %memory_back_kernel.1 = (bf16[2,3,224,1024]{3,2,1,0:T(8,128)(2,1)}, f32[2,3,224,1024]{3,2,1,0:T(8,128)}) custom-call(bf16[896,512]{1,0:T(8,128)(2,1)} %get-tuple-element.206.refs_4_.refs_0_, bf16[896,512]{1,0:T(8,128)(2,1)} %get-tuple-element.207.refs_5_.refs_1_, bf16[896,512]{1,0:T(8,128)(2,1)} %get-tuple-element.208.refs_6_.refs_2_, bf16[1024,768]{1,0:T(8,128)(2,1)} %bitcast.70), custom_call_target="tpu_custom_call" | custom-call | flops 8800000000 | tf_op jit(solution)/shard_map/memory_back_kernel/pallas_call | solution.py:140
  374.4 4.7 collective-permute-done.45
  379.0 3.6 add_convert_fusion.1
  386.7 15.8 %collective-permute-done.44.arrived = bf16[4,144,1024]{2,1,0:T(8,128)(2,1)} collective-permute-done((bf16[4,144,1024]{2,1,0:T(8,128)(2,1)}, bf16[4,144,1024]{2,1,0:T(8,128)(2,1)}, u32[]{:S(2)}, u32[]{:S(2)}) %collective-permute-start.44) | collective-permute-done | bytes 1179680 | tf_op jit(solution)/shard_map/ppermute | solution.py:40
  407.7 8.3 %collective-permute-done.46 = bf16[1,3,224,1024]{3,2,1,0:T(8,128)(2,1)S(1)} collective-permute-done((bf16[1,3,224,1024]{3,2,1,0:T(8,128)(2,1)}, bf16[1,3,224,1024]{3,2,1,0:T(8,128)(2,1)S(1)}, u32[]{:S(2)}, u32[]{:S(2)}) %collective-permute-start.46) | collective-permute-done | bytes 1376288 | tf_op jit(solution)/shard_map/ppermute | solution.py:40
  415.9 2.8 pair_sum_kernel.3
  420.1 2.4 collective-permute-start.49
  427.3 3.6 collective-permute-done.47.refs_0_
  430.9 10.3 %collective-permute-done.48.refs_1_ = bf16[144,1024]{1,0:T(8,128)(2,1)} collective-permute-done((bf16[144,1024]{1,0:T(8,128)(2,1)}, bf16[144,1024]{1,0:T(8,128)(2,1)}, u32[]{:S(2)}, u32[]{:S(2)}) %collective-permute-start.48) | collective-permute-done | bytes 294944 | tf_op jit(solution)/shard_map/ppermute | solution.py:720
  445.6 8.2 %collective-permute-start.50 = (bf16[128,512]{1,0:T(8,128)(2,1)S(1)}, bf16[128,512]{1,0:T(8,128)(2,1)S(1)}, u32[]{:S(2)}, u32[]{:S(2)}) collective-permute-start(bf16[128,512]{1,0:T(8,128)(2,1)S(1)} %pad_maximum_fusion.1), channel_id=1, source_target_pairs={{0,0},{1,4},{2,8},{3,12},{4,16},{5,20},{6,24},{7,28},{8,1},{9,5},{... | collective-permute-start | bytes 393224 | tf_op jit(solution)/shard_map/ppermute | solution.py:861
  453.9 3.6 add_convert_fusion
  457.8 4.8 collective-permute-start.51
  467.3 5.7 %collective-permute-start.54 = (bf16[3,32,1024]{2,1,0:T(8,128)(2,1)S(1)}, bf16[3,32,1024]{2,1,0:T(8,128)(2,1)S(1)}, u32[]{:S(2)}, u32[]{:S(2)}) collective-permute-start(bf16[3,32,1024]{2,1,0:T(8,128)(2,1)S(1)} %bitcast.46), channel_id=1, source_target_pairs={{0,0},{1,8},{2,4},{3,12},{4,2},{5,10},{6,6},{7,14},{8,1},{9,9},{10... | collective-permute-start | bytes 589832 | tf_op jit(solution)/shard_map/ppermute | solution.py:717
  473.1 8.0 %collective-permute-done.54 = bf16[3,32,1024]{2,1,0:T(8,128)(2,1)S(1)} collective-permute-done((bf16[3,32,1024]{2,1,0:T(8,128)(2,1)S(1)}, bf16[3,32,1024]{2,1,0:T(8,128)(2,1)S(1)}, u32[]{:S(2)}, u32[]{:S(2)}) %collective-permute-start.54) | collective-permute-done | bytes 196640 | tf_op jit(solution)/shard_map/ppermute | solution.py:717
  483.1 2.9 collective-permute-start.59
  491.1 8.5 %collective-permute-done.59.refs_4_ = bf16[144,2048]{1,0:T(8,128)(2,1)} collective-permute-done((bf16[144,2048]{1,0:T(8,128)(2,1)}, bf16[144,2048]{1,0:T(8,128)(2,1)}, u32[]{:S(2)}, u32[]{:S(2)}) %collective-permute-start.59) | collective-permute-done | bytes 589856 | tf_op jit(solution)/shard_map/ppermute | solution.py:40
  499.6 2.9 collective-permute-start.60
  502.4 9.7 %collective-permute-done.61.refs_6_ = bf16[144,2048]{1,0:T(8,128)(2,1)} collective-permute-done((bf16[144,2048]{1,0:T(8,128)(2,1)S(1)}, bf16[144,2048]{1,0:T(8,128)(2,1)}, u32[]{:S(2)}, u32[]{:S(2)}) %collective-permute-start.61) | collective-permute-done | bytes 589856 | tf_op jit(solution)/shard_map/ppermute | solution.py:40
  513.1 6.1 %ffn_out_kernel.1 = (f32[256,4096]{1,0:T(8,128)}, f32[1024,1024]{1,0:T(8,128)}) custom-call(bf16[128,2048]{1,0:T(8,128)(2,1)} %reduce-scatter.2.cloned.1.call-done.refs_0_, bf16[128,2048]{1,0:T(8,128)(2,1)} %collective-permute-done.63.refs_1_, bf16[128,2048]{1,0:T(8,128)(2,1)} %collective-permute-done.64.refs_2_, bf16[128,2048]{1,0:T(8,128)(2,1)} %copy-done.12, ...), custom_call_target="tpu_custom_call" | custom-call | flops 6600000000 | tf_op jit(solution)/shard_map/ffn_out_kernel/pallas_call | solution.py:140
  520.0 10.9 %collective-permute-done.55 = bf16[3,7,32,1024]{3,2,1,0:T(8,128)(2,1)S(1)} collective-permute-done((bf16[3,7,32,1024]{3,2,1,0:T(8,128)(2,1)S(1)}, bf16[3,7,32,1024]{3,2,1,0:T(8,128)(2,1)S(1)}, u32[]{:S(2)}, u32[]{:S(2)}) %collective-permute-start.55) | collective-permute-done | bytes 1376288 | tf_op jit(solution)/shard_map/ppermute | solution.py:717
  530.9 6.0 %proj_out_kernel.1 = (f32[6,256,1024]{2,1,0:T(8,128)}, f32[2,256,1024]{2,1,0:T(8,128)}, f32[6,256]{1,0:T(8,128)}, f32[1,256]{1,0:T(1,128)}, f32[1,1024]{1,0:T(1,128)}, /*index=5*/f32[6,256]{1,0:T(8,128)}) custom-call(bf16[144,2048]{1,0:T(8,128)(2,1)} %join_kernel.1.refs_0_, bf16[144,2048]{1,0:T(8,128)(2,1)} %collective-permute-done.56.refs_1_, ...), custom_call_target="tpu_custom_call" | custom-call | flops 7699999744 | tf_op jit(solution)/shard_map/proj_out_kernel/pallas_call | solution.py:140
  (281 shorter events, 92.6 us)
Async XLA Ops:
  7.2 136.1 %all-gather.5.cloned.1.call-start = ((), (), s32[]{:S(2)}) async-start(), calls=%async_computation.2 | async-start | bytes 4718592 | tf_op jit(solution)/shard_map/all_gather | solution.py:775
  7.2 12.9 %collective-permute-start = (bf16[3,32,1024]{2,1,0:T(8,128)(2,1)}, bf16[3,32,1024]{2,1,0:T(8,128)(2,1)S(1)}, u32[]{:S(2)}, u32[]{:S(2)}) collective-permute-start(bf16[3,32,1024]{2,1,0:T(8,128)(2,1)} %param.16), channel_id=1, source_target_pairs={{0,0},{1,8},{2,4},{3,12},{4,2},{5,10},{6,6},{7,14},{8,1},{9,9},{10... | collective-permute-start | bytes 589832 | tf_op jit(solution)/shard_map/ppermute | solution.py:717
  12.1 8.0 %collective-permute-start.1 = (s32[3,1024]{1,0:T(4,128)S(1)}, s32[3,1024]{1,0:T(4,128)S(1)}, u32[]{:S(2)}, u32[]{:S(2)}) collective-permute-start(s32[3,1024]{1,0:T(4,128)S(1)} %pad_add_fusion), channel_id=1, source_target_pairs={{0,0},{1,8},{2,4},{3,12},{4,2},{5,10},{6,6},{7,14},{8,1},{9,9},{10... | collective-permute-start | bytes 36872 | tf_op jit(solution)/shard_map/ppermute | solution.py:717
  20.1 37.8 %collective-permute-start.2 = (bf16[2,7,32,1024]{3,2,1,0:T(8,128)(2,1)S(1)}, bf16[2,7,32,1024]{3,2,1,0:T(8,128)(2,1)S(1)}, u32[]{:S(2)}, u32[]{:S(2)}) collective-permute-start(bf16[2,7,32,1024]{3,2,1,0:T(8,128)(2,1)S(1)} %slice.77), channel_id=1, source_target_pairs={{0,0},{1,8},{2,4},{3,12},{4,2},{5,10},{6,6},{7,14},{8,1},{9,9},{10... | collective-permute-start | bytes 2752520 | tf_op jit(solution)/shard_map/ppermute | solution.py:717
  24.1 3.8 collective-permute-start.9
  26.5 10.8 %collective-permute-start.10 = (bf16[32,2560]{1,0:T(8,128)(2,1)}, bf16[32,2560]{1,0:T(8,128)(2,1)S(1)}, u32[]{:S(2)}, u32[]{:S(2)}) collective-permute-start(bf16[32,2560]{1,0:T(8,128)(2,1)} %get-tuple-element.132), channel_id=1, source_target_pairs={{0,8},{8,0},{1,9},{9,1},{2,10},{10,2},{3,11},{11,3},{4,12},{12,4},... | collective-permute-start | bytes 491528 | tf_op jit(solution)/shard_map/ppermute | solution.py:40
  26.5 28.6 %collective-permute-start.11 = (bf16[32,2560]{1,0:T(8,128)(2,1)}, bf16[32,2560]{1,0:T(8,128)(2,1)S(1)}, u32[]{:S(2)}, u32[]{:S(2)}) collective-permute-start(bf16[32,2560]{1,0:T(8,128)(2,1)} %get-tuple-element.133), channel_id=1, source_target_pairs={{0,12},{4,8},{8,4},{12,0},{1,13},{5,9},{9,5},{13,1},{2,14},{6,10},... | collective-permute-start | bytes 491528 | tf_op jit(solution)/shard_map/ppermute | solution.py:765
  57.9 160.5 %all-gather.7.cloned.1.call-start = ((), (), s32[]{:S(2)}) async-start(), calls=%async_computation.3 | async-start | bytes 4718592 | tf_op jit(solution)/shard_map/all_gather | solution.py:785
  59.0 39.5 %collective-permute-start.3 = (bf16[1,7,32,1024]{3,2,1,0:T(8,128)(2,1)S(1)}, bf16[1,7,32,1024]{3,2,1,0:T(8,128)(2,1)S(1)}, u32[]{:S(2)}, u32[]{:S(2)}) collective-permute-start(bf16[1,7,32,1024]{3,2,1,0:T(8,128)(2,1)S(1)} %slice.78), channel_id=1, source_target_pairs={{0,0},{1,8},{2,4},{3,12},{4,2},{5,10},{6,6},{7,14},{8,1},{9,9},{10... | collective-permute-start | bytes 1376264 | tf_op jit(solution)/shard_map/ppermute | solution.py:717
  98.7 24.1 %collective-permute-start.4 = (bf16[3,224,1024]{2,1,0:T(8,128)(2,1)S(1)}, bf16[3,224,1024]{2,1,0:T(8,128)(2,1)}, u32[]{:S(2)}, u32[]{:S(2)}) collective-permute-start(bf16[3,224,1024]{2,1,0:T(8,128)(2,1)S(1)} %bitcast.41), channel_id=1, source_target_pairs={{0,8},{8,0},{1,9},{9,1},{2,10},{10,2},{3,11},{11,3},{4,12},{12,4},... | collective-permute-start | bytes 4128776 | tf_op jit(solution)/shard_map/ppermute | solution.py:40
  98.8 12.1 %collective-permute-start.23 = (bf16[128,1024]{1,0:T(8,128)(2,1)S(1)}, bf16[128,1024]{1,0:T(8,128)(2,1)S(1)}, u32[]{:S(2)}, u32[]{:S(2)}) collective-permute-start(bf16[128,1024]{1,0:T(8,128)(2,1)S(1)} %copy-done.15), channel_id=1, source_target_pairs={{0,0},{1,1},{2,4},{3,5},{4,8},{5,9},{6,12},{7,13},{8,2},{9,3},{10,... | collective-permute-start | bytes 786440 | tf_op jit(solution)/shard_map/ppermute | solution.py:773
  113.7 247.3 %reduce-scatter.2.cloned.1.call-start = ((), (), s32[]{:S(2)}) async-start(), calls=%async_computation.1 | async-start | bytes 4718592 | tf_op jit(solution)/shard_map/reduce_scatter | solution.py:930
  122.8 9.4 %collective-permute-start.5 = (bf16[3,224,1024]{2,1,0:T(8,128)(2,1)}, bf16[3,224,1024]{2,1,0:T(8,128)(2,1)}, u32[]{:S(2)}, u32[]{:S(2)}) collective-permute-start(bf16[3,224,1024]{2,1,0:T(8,128)(2,1)} %collective-permute-done.4.m1.refs_1_), channel_id=1, source_target_pairs={{0,4},{4,0},{1,5},{5,1},{2,6},{6,2},{3,7},{7,3},{8,12},{12,8},{9,1... | collective-permute-start | bytes 4128776 | tf_op jit(solution)/shard_map/ppermute | solution.py:40
  123.3 7.4 %collective-permute-start.6 = (bf16[96,1024]{1,0:T(8,128)(2,1)S(1)}, bf16[96,1024]{1,0:T(8,128)(2,1)S(1)}, u32[]{:S(2)}, u32[]{:S(2)}) collective-permute-start(bf16[96,1024]{1,0:T(8,128)(2,1)S(1)} %bitcast.55), channel_id=1, source_target_pairs={{0,8},{8,0},{1,9},{9,1},{2,10},{10,2},{3,11},{11,3},{4,12},{12,4},... | collective-permute-start | bytes 589832 | tf_op jit(solution)/shard_map/ppermute | solution.py:40
  123.5 8.7 %collective-permute-start.7 = (bf16[96,1024]{1,0:T(8,128)(2,1)S(1)}, bf16[96,1024]{1,0:T(8,128)(2,1)S(1)}, u32[]{:S(2)}, u32[]{:S(2)}) collective-permute-start(bf16[96,1024]{1,0:T(8,128)(2,1)S(1)} %bitcast.56), channel_id=1, source_target_pairs={{0,4},{4,0},{1,5},{5,1},{2,6},{6,2},{3,7},{7,3},{8,12},{12,8},{9,1... | collective-permute-start | bytes 589832 | tf_op jit(solution)/shard_map/ppermute | solution.py:40
  131.6 41.0 %collective-permute-start.17 = (bf16[3,224,1024]{2,1,0:T(8,128)(2,1)S(1)}, bf16[3,224,1024]{2,1,0:T(8,128)(2,1)}, u32[]{:S(2)}, u32[]{:S(2)}) collective-permute-start(bf16[3,224,1024]{2,1,0:T(8,128)(2,1)S(1)} %bitcast.42), channel_id=1, source_target_pairs={{0,4},{4,0},{1,5},{5,1},{2,6},{6,2},{3,7},{7,3},{8,12},{12,8},{9,1... | collective-permute-start | bytes 4128776 | tf_op jit(solution)/shard_map/ppermute | solution.py:40
  155.9 7.0 %collective-permute-start.13 = (bf16[96,1024]{1,0:T(8,128)(2,1)S(1)}, bf16[96,1024]{1,0:T(8,128)(2,1)S(1)}, u32[]{:S(2)}, u32[]{:S(2)}) collective-permute-start(bf16[96,1024]{1,0:T(8,128)(2,1)S(1)} %add_convert_fusion.8), channel_id=1, source_target_pairs={{0,8},{8,0},{1,9},{9,1},{2,10},{10,2},{3,11},{11,3},{4,12},{12,4},... | collective-permute-start | bytes 589832 | tf_op jit(solution)/shard_map/ppermute | solution.py:40
  166.1 6.4 %collective-permute-start.14 = (bf16[96,1024]{1,0:T(8,128)(2,1)}, bf16[96,1024]{1,0:T(8,128)(2,1)S(1)}, u32[]{:S(2)}, u32[]{:S(2)}) collective-permute-start(bf16[96,1024]{1,0:T(8,128)(2,1)} %get-tuple-element.139.refs_0_.h0), channel_id=1, source_target_pairs={{0,8},{8,0},{1,9},{9,1},{2,10},{10,2},{3,11},{11,3},{4,12},{12,4},... | collective-permute-start | bytes 589832 | tf_op jit(solution)/shard_map/ppermute | solution.py:40
  167.3 12.4 %collective-permute-start.15 = (bf16[96,1024]{1,0:T(8,128)(2,1)}, bf16[96,1024]{1,0:T(8,128)(2,1)S(1)}, u32[]{:S(2)}, u32[]{:S(2)}) collective-permute-start(bf16[96,1024]{1,0:T(8,128)(2,1)} %get-tuple-element.139.refs_0_.h0), channel_id=1, source_target_pairs={{0,4},{4,0},{1,5},{5,1},{2,6},{6,2},{3,7},{7,3},{8,12},{12,8},{9,1... | collective-permute-start | bytes 589832 | tf_op jit(solution)/shard_map/ppermute | solution.py:40
  172.5 7.2 %collective-permute-start.16 = (bf16[96,1024]{1,0:T(8,128)(2,1)S(1)}, bf16[96,1024]{1,0:T(8,128)(2,1)S(1)}, u32[]{:S(2)}, u32[]{:S(2)}) collective-permute-start(bf16[96,1024]{1,0:T(8,128)(2,1)S(1)} %collective-permute-done.14.refs_1_.h1), channel_id=1, source_target_pairs={{0,4},{4,0},{1,5},{5,1},{2,6},{6,2},{3,7},{7,3},{8,12},{12,8},{9,1... | collective-permute-start | bytes 589832 | tf_op jit(solution)/shard_map/ppermute | solution.py:40
  191.6 7.2 %collective-permute-start.19 = (bf16[96,1024]{1,0:T(8,128)(2,1)S(1)}, bf16[96,1024]{1,0:T(8,128)(2,1)S(1)}, u32[]{:S(2)}, u32[]{:S(2)}) collective-permute-start(bf16[96,1024]{1,0:T(8,128)(2,1)S(1)} %add_convert_fusion.7), channel_id=1, source_target_pairs={{0,8},{8,0},{1,9},{9,1},{2,10},{10,2},{3,11},{11,3},{4,12},{12,4},... | collective-permute-start | bytes 589832 | tf_op jit(solution)/shard_map/ppermute | solution.py:40
  202.1 6.7 %collective-permute-start.20 = (bf16[96,1024]{1,0:T(8,128)(2,1)}, bf16[96,1024]{1,0:T(8,128)(2,1)S(1)}, u32[]{:S(2)}, u32[]{:S(2)}) collective-permute-start(bf16[96,1024]{1,0:T(8,128)(2,1)} %get-tuple-element.148.h0.a0), channel_id=1, source_target_pairs={{0,8},{8,0},{1,9},{9,1},{2,10},{10,2},{3,11},{11,3},{4,12},{12,4},... | collective-permute-start | bytes 589832 | tf_op jit(solution)/shard_map/ppermute | solution.py:40
  202.7 20.2 %collective-permute-start.21 = (bf16[96,1024]{1,0:T(8,128)(2,1)}, bf16[96,1024]{1,0:T(8,128)(2,1)S(1)}, u32[]{:S(2)}, u32[]{:S(2)}) collective-permute-start(bf16[96,1024]{1,0:T(8,128)(2,1)} %get-tuple-element.148.h0.a0), channel_id=1, source_target_pairs={{0,4},{4,0},{1,5},{5,1},{2,6},{6,2},{3,7},{7,3},{8,12},{12,8},{9,1... | collective-permute-start | bytes 589832 | tf_op jit(solution)/shard_map/ppermute | solution.py:40
  208.8 14.1 %collective-permute-start.22 = (bf16[96,1024]{1,0:T(8,128)(2,1)S(1)}, bf16[96,1024]{1,0:T(8,128)(2,1)S(1)}, u32[]{:S(2)}, u32[]{:S(2)}) collective-permute-start(bf16[96,1024]{1,0:T(8,128)(2,1)S(1)} %collective-permute-done.20.h1.a1), channel_id=1, source_target_pairs={{0,4},{4,0},{1,5},{5,1},{2,6},{6,2},{3,7},{7,3},{8,12},{12,8},{9,1... | collective-permute-start | bytes 589832 | tf_op jit(solution)/shard_map/ppermute | solution.py:40
  230.0 12.8 %collective-permute-start.26 = (bf16[3,32,1024]{2,1,0:T(8,128)(2,1)S(1)}, bf16[3,32,1024]{2,1,0:T(8,128)(2,1)S(1)}, u32[]{:S(2)}, u32[]{:S(2)}) collective-permute-start(bf16[3,32,1024]{2,1,0:T(8,128)(2,1)S(1)} %copy-done.23), channel_id=1, source_target_pairs={{0,0},{1,8},{2,4},{3,12},{4,2},{5,10},{6,6},{7,14},{8,1},{9,9},{10... | collective-permute-start | bytes 589832 | tf_op jit(solution)/shard_map/ppermute | solution.py:717
  233.9 11.7 %collective-permute-start.25 = (bf16[96,1024]{1,0:T(8,128)(2,1)S(1)}, bf16[96,1024]{1,0:T(8,128)(2,1)S(1)}, u32[]{:S(2)}, u32[]{:S(2)}) collective-permute-start(bf16[96,1024]{1,0:T(8,128)(2,1)S(1)} %add_convert_fusion.6), channel_id=1, source_target_pairs={{0,8},{8,0},{1,9},{9,1},{2,10},{10,2},{3,11},{11,3},{4,12},{12,4},... | collective-permute-start | bytes 589832 | tf_op jit(solution)/shard_map/ppermute | solution.py:40
  249.2 7.0 %collective-permute-start.27 = (bf16[96,1024]{1,0:T(8,128)(2,1)}, bf16[96,1024]{1,0:T(8,128)(2,1)S(1)}, u32[]{:S(2)}, u32[]{:S(2)}) collective-permute-start(bf16[96,1024]{1,0:T(8,128)(2,1)} %get-tuple-element.158.f0), channel_id=1, source_target_pairs={{0,8},{8,0},{1,9},{9,1},{2,10},{10,2},{3,11},{11,3},{4,12},{12,4},... | collective-permute-start | bytes 589832 | tf_op jit(solution)/shard_map/ppermute | solution.py:40
  249.2 7.0 %collective-permute-start.28 = (bf16[96,1024]{1,0:T(8,128)(2,1)}, bf16[96,1024]{1,0:T(8,128)(2,1)S(1)}, u32[]{:S(2)}, u32[]{:S(2)}) collective-permute-start(bf16[96,1024]{1,0:T(8,128)(2,1)} %get-tuple-element.158.f0), channel_id=1, source_target_pairs={{0,4},{4,0},{1,5},{5,1},{2,6},{6,2},{3,7},{7,3},{8,12},{12,8},{9,1... | collective-permute-start | bytes 589832 | tf_op jit(solution)/shard_map/ppermute | solution.py:40
  273.6 7.0 %collective-permute-start.31 = (bf16[96,1024]{1,0:T(8,128)(2,1)S(1)}, bf16[96,1024]{1,0:T(8,128)(2,1)S(1)}, u32[]{:S(2)}, u32[]{:S(2)}) collective-permute-start(bf16[96,1024]{1,0:T(8,128)(2,1)S(1)} %add_convert_fusion.5), channel_id=1, source_target_pairs={{0,8},{8,0},{1,9},{9,1},{2,10},{10,2},{3,11},{11,3},{4,12},{12,4},... | collective-permute-start | bytes 589832 | tf_op jit(solution)/shard_map/ppermute | solution.py:40
  284.0 6.4 %collective-permute-start.32 = (bf16[96,1024]{1,0:T(8,128)(2,1)}, bf16[96,1024]{1,0:T(8,128)(2,1)S(1)}, u32[]{:S(2)}, u32[]{:S(2)}) collective-permute-start(bf16[96,1024]{1,0:T(8,128)(2,1)} %get-tuple-element.167.refs_0_.f0), channel_id=1, source_target_pairs={{0,8},{8,0},{1,9},{9,1},{2,10},{10,2},{3,11},{11,3},{4,12},{12,4},... | collective-permute-start | bytes 589832 | tf_op jit(solution)/shard_map/ppermute | solution.py:40
  284.3 6.2 %collective-permute-start.33 = (bf16[96,1024]{1,0:T(8,128)(2,1)}, bf16[96,1024]{1,0:T(8,128)(2,1)S(1)}, u32[]{:S(2)}, u32[]{:S(2)}) collective-permute-start(bf16[96,1024]{1,0:T(8,128)(2,1)} %get-tuple-element.167.refs_0_.f0), channel_id=1, source_target_pairs={{0,4},{4,0},{1,5},{5,1},{2,6},{6,2},{3,7},{7,3},{8,12},{12,8},{9,1... | collective-permute-start | bytes 589832 | tf_op jit(solution)/shard_map/ppermute | solution.py:40
  306.4 7.2 %collective-permute-start.37 = (bf16[96,1024]{1,0:T(8,128)(2,1)S(1)}, bf16[96,1024]{1,0:T(8,128)(2,1)S(1)}, u32[]{:S(2)}, u32[]{:S(2)}) collective-permute-start(bf16[96,1024]{1,0:T(8,128)(2,1)S(1)} %add_convert_fusion.4), channel_id=1, source_target_pairs={{0,8},{8,0},{1,9},{9,1},{2,10},{10,2},{3,11},{11,3},{4,12},{12,4},... | collective-permute-start | bytes 589832 | tf_op jit(solution)/shard_map/ppermute | solution.py:40
  317.0 9.2 %collective-permute-start.38 = (bf16[96,1024]{1,0:T(8,128)(2,1)}, bf16[96,1024]{1,0:T(8,128)(2,1)S(1)}, u32[]{:S(2)}, u32[]{:S(2)}) collective-permute-start(bf16[96,1024]{1,0:T(8,128)(2,1)} %get-tuple-element.183.f0), channel_id=1, source_target_pairs={{0,8},{8,0},{1,9},{9,1},{2,10},{10,2},{3,11},{11,3},{4,12},{12,4},... | collective-permute-start | bytes 589832 | tf_op jit(solution)/shard_map/ppermute | solution.py:40
  326.1 6.8 %collective-permute-start.39 = (bf16[96,1024]{1,0:T(8,128)(2,1)S(1)}, bf16[96,1024]{1,0:T(8,128)(2,1)S(1)}, u32[]{:S(2)}, u32[]{:S(2)}) collective-permute-start(bf16[96,1024]{1,0:T(8,128)(2,1)S(1)} %copy-done.37), channel_id=1, source_target_pairs={{0,4},{4,0},{1,5},{5,1},{2,6},{6,2},{3,7},{7,3},{8,12},{12,8},{9,1... | collective-permute-start | bytes 589832 | tf_op jit(solution)/shard_map/ppermute | solution.py:40
  326.2 6.8 %collective-permute-start.40 = (bf16[96,1024]{1,0:T(8,128)(2,1)S(1)}, bf16[96,1024]{1,0:T(8,128)(2,1)S(1)}, u32[]{:S(2)}, u32[]{:S(2)}) collective-permute-start(bf16[96,1024]{1,0:T(8,128)(2,1)S(1)} %collective-permute-done.38.f1), channel_id=1, source_target_pairs={{0,4},{4,0},{1,5},{5,1},{2,6},{6,2},{3,7},{7,3},{8,12},{12,8},{9,1... | collective-permute-start | bytes 589832 | tf_op jit(solution)/shard_map/ppermute | solution.py:40
  330.8 31.1 %collective-permute-start.35 = (bf16[4,128,1024]{2,1,0:T(8,128)(2,1)}, bf16[4,128,1024]{2,1,0:T(8,128)(2,1)S(1)}, u32[]{:S(2)}, u32[]{:S(2)}) collective-permute-start(bf16[4,128,1024]{2,1,0:T(8,128)(2,1)} %get-tuple-element.177), channel_id=1, source_target_pairs={{0,16},{16,0},{1,17},{17,1},{2,18},{18,2},{3,19},{19,3},{4,20},{20... | collective-permute-start | bytes 3145736 | tf_op jit(solution)/shard_map/ppermute | solution.py:40
  373.7 5.3 collective-permute-start.45
  373.7 28.7 %collective-permute-start.44 = (bf16[4,144,1024]{2,1,0:T(8,128)(2,1)}, bf16[4,144,1024]{2,1,0:T(8,128)(2,1)}, u32[]{:S(2)}, u32[]{:S(2)}) collective-permute-start(bf16[4,144,1024]{2,1,0:T(8,128)(2,1)} %get-tuple-element.205), channel_id=1, source_target_pairs={{0,16},{16,0},{1,17},{17,1},{2,18},{18,2},{3,19},{19,3},{4,20},{20... | collective-permute-start | bytes 3538952 | tf_op jit(solution)/shard_map/ppermute | solution.py:40
  382.7 33.2 %collective-permute-start.46 = (bf16[1,3,224,1024]{3,2,1,0:T(8,128)(2,1)}, bf16[1,3,224,1024]{3,2,1,0:T(8,128)(2,1)S(1)}, u32[]{:S(2)}, u32[]{:S(2)}) collective-permute-start(bf16[1,3,224,1024]{3,2,1,0:T(8,128)(2,1)} %add_convert_fusion.1), channel_id=1, source_target_pairs={{0,8},{8,0},{1,9},{9,1},{2,10},{10,2},{3,11},{11,3},{4,12},{12,4},... | collective-permute-start | bytes 4128776 | tf_op jit(solution)/shard_map/ppermute | solution.py:40
  384.4 18.1 %collective-permute-start.42 = (bf16[128,1024]{1,0:T(8,128)(2,1)S(1)}, bf16[128,1024]{1,0:T(8,128)(2,1)S(1)}, u32[]{:S(2)}, u32[]{:S(2)}) collective-permute-start(bf16[128,1024]{1,0:T(8,128)(2,1)S(1)} %copy-done.18), channel_id=1, source_target_pairs={{0,2},{1,3},{2,0},{3,1},{4,6},{5,7},{6,4},{7,5},{8,10},{9,11},{10,... | collective-permute-start | bytes 786440 | tf_op jit(solution)/shard_map/ppermute | solution.py:720
  384.6 19.1 %collective-permute-start.43 = (bf16[128,1024]{1,0:T(8,128)(2,1)S(1)}, bf16[128,1024]{1,0:T(8,128)(2,1)S(1)}, u32[]{:S(2)}, u32[]{:S(2)}) collective-permute-start(bf16[128,1024]{1,0:T(8,128)(2,1)S(1)} %copy-done.17), channel_id=1, source_target_pairs={{0,3},{1,0},{2,1},{3,2},{4,7},{5,4},{6,5},{7,6},{8,11},{9,8},{10,9... | collective-permute-start | bytes 786440 | tf_op jit(solution)/shard_map/ppermute | solution.py:720
  386.1 18.7 %collective-permute-start.41 = (bf16[128,1024]{1,0:T(8,128)(2,1)S(1)}, bf16[128,1024]{1,0:T(8,128)(2,1)S(1)}, u32[]{:S(2)}, u32[]{:S(2)}) collective-permute-start(bf16[128,1024]{1,0:T(8,128)(2,1)S(1)} %copy-done.16), channel_id=1, source_target_pairs={{0,1},{1,2},{2,3},{3,0},{4,5},{5,6},{6,7},{7,4},{8,9},{9,10},{10,1... | collective-permute-start | bytes 786440 | tf_op jit(solution)/shard_map/ppermute | solution.py:720
  402.4 17.7 %collective-permute-start.52 = (bf16[192,1024]{1,0:T(8,128)(2,1)}, bf16[192,1024]{1,0:T(8,128)(2,1)}, u32[]{:S(2)}, u32[]{:S(2)}) collective-permute-start(bf16[192,1024]{1,0:T(8,128)(2,1)} %get-tuple-element.219), channel_id=1, source_target_pairs={{0,4},{4,0},{1,5},{5,1},{2,6},{6,2},{3,7},{7,3},{8,12},{12,8},{9,1... | collective-permute-start | bytes 1179656 | tf_op jit(solution)/shard_map/ppermute | solution.py:40
  402.4 21.9 %collective-permute-start.66 = (bf16[128,2048]{1,0:T(8,128)(2,1)}, bf16[128,2048]{1,0:T(8,128)(2,1)}, u32[]{:S(2)}, u32[]{:S(2)}) collective-permute-start(bf16[128,2048]{1,0:T(8,128)(2,1)} %reduce-scatter.2.cloned.1.call-done.refs_0_), channel_id=1, source_target_pairs={{0,16},{16,0},{1,17},{17,1},{2,18},{18,2},{3,19},{19,3},{4,20},{20... | collective-permute-start | bytes 1572872 | tf_op jit(solution)/shard_map/ppermute | solution.py:40
  403.7 23.5 %collective-permute-start.64 = (bf16[128,2048]{1,0:T(8,128)(2,1)}, bf16[128,2048]{1,0:T(8,128)(2,1)}, u32[]{:S(2)}, u32[]{:S(2)}) collective-permute-start(bf16[128,2048]{1,0:T(8,128)(2,1)} %reduce-scatter.2.cloned.1.call-done.refs_0_), channel_id=1, source_target_pairs={{0,8},{8,0},{1,9},{9,1},{2,10},{10,2},{3,11},{11,3},{4,12},{12,4},... | collective-permute-start | bytes 1572872 | tf_op jit(solution)/shard_map/ppermute | solution.py:40
  418.7 12.2 %collective-permute-start.47 = (bf16[144,1024]{1,0:T(8,128)(2,1)}, bf16[144,1024]{1,0:T(8,128)(2,1)}, u32[]{:S(2)}, u32[]{:S(2)}) collective-permute-start(bf16[144,1024]{1,0:T(8,128)(2,1)} %get-tuple-element.213), channel_id=1, source_target_pairs={{0,1},{1,2},{2,3},{3,0},{4,5},{5,6},{6,7},{7,4},{8,9},{9,10},{10,1... | collective-permute-start | bytes 884744 | tf_op jit(solution)/shard_map/ppermute | solution.py:720
  419.2 22.0 %collective-permute-start.48 = (bf16[144,1024]{1,0:T(8,128)(2,1)}, bf16[144,1024]{1,0:T(8,128)(2,1)}, u32[]{:S(2)}, u32[]{:S(2)}) collective-permute-start(bf16[144,1024]{1,0:T(8,128)(2,1)} %get-tuple-element.214), channel_id=1, source_target_pairs={{0,2},{1,3},{2,0},{3,1},{4,6},{5,7},{6,4},{7,5},{8,10},{9,11},{10,... | collective-permute-start | bytes 884744 | tf_op jit(solution)/shard_map/ppermute | solution.py:720
  420.1 21.7 %collective-permute-start.49 = (bf16[144,1024]{1,0:T(8,128)(2,1)}, bf16[144,1024]{1,0:T(8,128)(2,1)}, u32[]{:S(2)}, u32[]{:S(2)}) collective-permute-start(bf16[144,1024]{1,0:T(8,128)(2,1)} %get-tuple-element.215), channel_id=1, source_target_pairs={{0,3},{1,0},{2,1},{3,2},{4,7},{5,4},{6,5},{7,6},{8,11},{9,8},{10,9... | collective-permute-start | bytes 884744 | tf_op jit(solution)/shard_map/ppermute | solution.py:720
  424.3 40.5 %collective-permute-start.53 = (bf16[96,1024]{1,0:T(8,128)(2,1)}, bf16[96,1024]{1,0:T(8,128)(2,1)}, u32[]{:S(2)}, u32[]{:S(2)}) collective-permute-start(bf16[96,1024]{1,0:T(8,128)(2,1)} %add_convert_fusion.3), channel_id=1, source_target_pairs={{0,8},{8,0},{1,9},{9,1},{2,10},{10,2},{3,11},{11,3},{4,12},{12,4},... | collective-permute-start | bytes 589832 | tf_op jit(solution)/shard_map/ppermute | solution.py:40
  427.3 55.8 %collective-permute-start.63 = (bf16[128,2048]{1,0:T(8,128)(2,1)}, bf16[128,2048]{1,0:T(8,128)(2,1)}, u32[]{:S(2)}, u32[]{:S(2)}) collective-permute-start(bf16[128,2048]{1,0:T(8,128)(2,1)} %reduce-scatter.2.cloned.1.call-done.refs_0_), channel_id=1, source_target_pairs={{0,4},{4,0},{1,5},{5,1},{2,6},{6,2},{3,7},{7,3},{8,12},{12,8},{9,1... | collective-permute-start | bytes 1572872 | tf_op jit(solution)/shard_map/ppermute | solution.py:40
  430.9 56.0 %collective-permute-start.67 = (bf16[128,2048]{1,0:T(8,128)(2,1)}, bf16[128,2048]{1,0:T(8,128)(2,1)}, u32[]{:S(2)}, u32[]{:S(2)}) collective-permute-start(bf16[128,2048]{1,0:T(8,128)(2,1)} %collective-permute-done.66.refs_4_), channel_id=1, source_target_pairs={{0,4},{4,0},{1,5},{5,1},{2,6},{6,2},{3,7},{7,3},{8,12},{12,8},{9,1... | collective-permute-start | bytes 1572872 | tf_op jit(solution)/shard_map/ppermute | solution.py:40
  441.2 47.0 %collective-permute-start.68 = (bf16[128,2048]{1,0:T(8,128)(2,1)}, bf16[128,2048]{1,0:T(8,128)(2,1)}, u32[]{:S(2)}, u32[]{:S(2)}) collective-permute-start(bf16[128,2048]{1,0:T(8,128)(2,1)} %collective-permute-done.64.refs_2_), channel_id=1, source_target_pairs={{0,16},{16,0},{1,17},{17,1},{2,18},{18,2},{3,19},{19,3},{4,20},{20... | collective-permute-start | bytes 1572872 | tf_op jit(solution)/shard_map/ppermute | solution.py:40
  445.6 12.2 %collective-permute-start.50 = (bf16[128,512]{1,0:T(8,128)(2,1)S(1)}, bf16[128,512]{1,0:T(8,128)(2,1)S(1)}, u32[]{:S(2)}, u32[]{:S(2)}) collective-permute-start(bf16[128,512]{1,0:T(8,128)(2,1)S(1)} %pad_maximum_fusion.1), channel_id=1, source_target_pairs={{0,0},{1,4},{2,8},{3,12},{4,16},{5,20},{6,24},{7,28},{8,1},{9,5},{... | collective-permute-start | bytes 393224 | tf_op jit(solution)/shard_map/ppermute | solution.py:861
  457.8 9.5 %collective-permute-start.51 = (bf16[3,32,1024]{2,1,0:T(8,128)(2,1)}, bf16[3,32,1024]{2,1,0:T(8,128)(2,1)S(1)}, u32[]{:S(2)}, u32[]{:S(2)}) collective-permute-start(bf16[3,32,1024]{2,1,0:T(8,128)(2,1)} %bitcast.17), channel_id=1, source_target_pairs={{0,0},{1,8},{2,4},{3,12},{4,2},{5,10},{6,6},{7,14},{8,1},{9,9},{10... | collective-permute-start | bytes 589832 | tf_op jit(solution)/shard_map/ppermute | solution.py:717
  464.8 21.1 %collective-permute-start.57 = (bf16[144,2048]{1,0:T(8,128)(2,1)}, bf16[144,2048]{1,0:T(8,128)(2,1)S(1)}, u32[]{:S(2)}, u32[]{:S(2)}) collective-permute-start(bf16[144,2048]{1,0:T(8,128)(2,1)} %join_kernel.1.refs_0_), channel_id=1, source_target_pairs={{0,8},{8,0},{1,9},{9,1},{2,10},{10,2},{3,11},{11,3},{4,12},{12,4},... | collective-permute-start | bytes 1769480 | tf_op jit(solution)/shard_map/ppermute | solution.py:40
  467.3 13.7 %collective-permute-start.54 = (bf16[3,32,1024]{2,1,0:T(8,128)(2,1)S(1)}, bf16[3,32,1024]{2,1,0:T(8,128)(2,1)S(1)}, u32[]{:S(2)}, u32[]{:S(2)}) collective-permute-start(bf16[3,32,1024]{2,1,0:T(8,128)(2,1)S(1)} %bitcast.46), channel_id=1, source_target_pairs={{0,0},{1,8},{2,4},{3,12},{4,2},{5,10},{6,6},{7,14},{8,1},{9,9},{10... | collective-permute-start | bytes 589832 | tf_op jit(solution)/shard_map/ppermute | solution.py:717
  481.1 49.8 %collective-permute-start.55 = (bf16[3,7,32,1024]{3,2,1,0:T(8,128)(2,1)S(1)}, bf16[3,7,32,1024]{3,2,1,0:T(8,128)(2,1)S(1)}, u32[]{:S(2)}, u32[]{:S(2)}) collective-permute-start(bf16[3,7,32,1024]{3,2,1,0:T(8,128)(2,1)S(1)} %bitcast.45), channel_id=1, source_target_pairs={{0,0},{1,8},{2,4},{3,12},{4,2},{5,10},{6,6},{7,14},{8,1},{9,9},{10... | collective-permute-start | bytes 4128776 | tf_op jit(solution)/shard_map/ppermute | solution.py:717
  483.1 16.5 %collective-permute-start.59 = (bf16[144,2048]{1,0:T(8,128)(2,1)}, bf16[144,2048]{1,0:T(8,128)(2,1)}, u32[]{:S(2)}, u32[]{:S(2)}) collective-permute-start(bf16[144,2048]{1,0:T(8,128)(2,1)} %join_kernel.1.refs_0_), channel_id=1, source_target_pairs={{0,16},{16,0},{1,17},{17,1},{2,18},{18,2},{3,19},{19,3},{4,20},{20... | collective-permute-start | bytes 1769480 | tf_op jit(solution)/shard_map/ppermute | solution.py:40
  486.0 26.1 %collective-permute-start.61 = (bf16[144,2048]{1,0:T(8,128)(2,1)S(1)}, bf16[144,2048]{1,0:T(8,128)(2,1)}, u32[]{:S(2)}, u32[]{:S(2)}) collective-permute-start(bf16[144,2048]{1,0:T(8,128)(2,1)S(1)} %collective-permute-done.57.refs_2_), channel_id=1, source_target_pairs={{0,16},{16,0},{1,17},{17,1},{2,18},{18,2},{3,19},{19,3},{4,20},{20... | collective-permute-start | bytes 1769480 | tf_op jit(solution)/shard_map/ppermute | solution.py:40
  486.9 3.0 collective-permute-start.65
  489.9 40.9 %collective-permute-start.56 = (bf16[144,2048]{1,0:T(8,128)(2,1)}, bf16[144,2048]{1,0:T(8,128)(2,1)}, u32[]{:S(2)}, u32[]{:S(2)}) collective-permute-start(bf16[144,2048]{1,0:T(8,128)(2,1)} %join_kernel.1.refs_0_), channel_id=1, source_target_pairs={{0,4},{4,0},{1,5},{5,1},{2,6},{6,2},{3,7},{7,3},{8,12},{12,8},{9,1... | collective-permute-start | bytes 1769480 | tf_op jit(solution)/shard_map/ppermute | solution.py:40
  490.7 40.2 %collective-permute-start.58 = (bf16[144,2048]{1,0:T(8,128)(2,1)S(1)}, bf16[144,2048]{1,0:T(8,128)(2,1)}, u32[]{:S(2)}, u32[]{:S(2)}) collective-permute-start(bf16[144,2048]{1,0:T(8,128)(2,1)S(1)} %collective-permute-done.57.refs_2_), channel_id=1, source_target_pairs={{0,4},{4,0},{1,5},{5,1},{2,6},{6,2},{3,7},{7,3},{8,12},{12,8},{9,1... | collective-permute-start | bytes 1769480 | tf_op jit(solution)/shard_map/ppermute | solution.py:40
  499.6 31.3 %collective-permute-start.60 = (bf16[144,2048]{1,0:T(8,128)(2,1)}, bf16[144,2048]{1,0:T(8,128)(2,1)}, u32[]{:S(2)}, u32[]{:S(2)}) collective-permute-start(bf16[144,2048]{1,0:T(8,128)(2,1)} %collective-permute-done.59.refs_4_), channel_id=1, source_target_pairs={{0,4},{4,0},{1,5},{5,1},{2,6},{6,2},{3,7},{7,3},{8,12},{12,8},{9,1... | collective-permute-start | bytes 1769480 | tf_op jit(solution)/shard_map/ppermute | solution.py:40
  512.1 18.7 %collective-permute-start.62 = (bf16[144,2048]{1,0:T(8,128)(2,1)}, bf16[144,2048]{1,0:T(8,128)(2,1)}, u32[]{:S(2)}, u32[]{:S(2)}) collective-permute-start(bf16[144,2048]{1,0:T(8,128)(2,1)} %collective-permute-done.61.refs_6_), channel_id=1, source_target_pairs={{0,4},{4,0},{1,5},{5,1},{2,6},{6,2},{3,7},{7,3},{8,12},{12,8},{9,1... | collective-permute-start | bytes 1769480 | tf_op jit(solution)/shard_map/ppermute | solution.py:40
  (65 other events, 582.5 us)
Sparse Core Ops, SparseCore 0:
  58.0 85.1 all-gather.4
  145.9 72.4 all-gather.6
  271.0 89.9 reduce-scatter.1
